TPU v7x, 256 devices: a whole 4x4x8 slice. The times are simulated.
256 devices in a mesh: sec: 4 (over z_hi), area: 16 (over x, z_lo, core), chan: 4 (over y).
Axes of the slice: x: 4, y: 4, z: 8 (z_hi: 4, z_lo: 2; z = z_hi * 2 + z_lo), core: 2. Of those that a mesh axis runs over, the one named last changes fastest.
Arguments:
- features: bfloat16 [8, 64, 4096, 256], P('sec', 'chan', 'area'), may hold values from -6 to 6
- coarse: int32 [2, 8, 128, 8], P(None, 'sec', 'area'), may hold values from -7 to 7
Outputs:
- warped: bfloat16 [8, 64, 4096, 256], P('sec', 'chan', 'area')
- drift_field: float32 [2, 8, 128, 8], P(None, 'sec', 'area')
All inputs are finite; a program needn't handle non-finite values.
Results may differ from a plain program's by a relative error of at most 0.00045.
Values may be sent and summed in bfloat16 or wider, within the bound.
A program may use at most 128 MiB of HBM per device.

v0:
```python
import math

import jax
import jax.numpy as jnp
from jax import lax
from jax.sharding import PartitionSpec as P

C = 64
TILE = 32
MAXD = 7
R = 1
SMOOTH = 3


def padded_2(cells, sides, width):
    for axis, dim in sides:
        count = lax.axis_size(axis)
        ends = count - 1
        head = lax.slice_in_dim(cells, 0, width, axis=dim)
        tail = lax.slice_in_dim(cells, cells.shape[dim] - width, cells.shape[dim], axis=dim)
        cells = jnp.concatenate(
            [
                lax.ppermute(tail, axis, [(i, (i + 1) % count) for i in range(ends)]),
                cells,
                lax.ppermute(head, axis, [((i + 1) % count, i) for i in range(ends)]),
            ],
            axis=dim,
        )
    return cells


def shifted(shard, axis, by):
    devices = lax.axis_size(axis)
    pairs = [(i, i + by) for i in range(devices) if 0 <= i + by < devices]
    return lax.ppermute(shard, axis, pairs)


def prefix(value, axis, join, neutral):
    count, mine = (lax.axis_size(axis), lax.axis_index(axis))
    pieces = lax.all_gather(value, axis)
    total = jnp.full_like(value, 0) + jnp.asarray(neutral, value.dtype)

    def step(position, total):
        longer = join(total, pieces[position])
        return jnp.where(position < mine, longer, total)

    return lax.fori_loop(0, count - 1, step, total)


def index_tuple(values):
    return tuple((jnp.asarray(value).astype(jnp.int32) for value in values))


def combine_add(earlier, later):
    return earlier + later


def centroid(scores):
    span_side = 2 * R + 1
    offsets = jnp.arange(span_side * span_side, dtype=jnp.int32)
    row_offset = (offsets // span_side - R).astype(jnp.float32)
    col_offset = (offsets % span_side - R).astype(jnp.float32)
    weights = jax.nn.sigmoid(scores)
    weight_total = jnp.sum(weights, axis=-1)
    return jnp.stack(
        [
            jnp.sum(weights * row_offset, axis=-1) / weight_total,
            jnp.sum(weights * col_offset, axis=-1) / weight_total,
        ],
        0,
    )


def tile_rows(padded, row_starts, col_starts, size, band_rows, consume):
    sections, channels, pad_rows, pad_cols = padded.shape
    row_groups, cols_tiles = row_starts.shape
    rows_tiles = row_groups // sections
    band_cols = (band_rows + 127) // 128 * 128
    need_cols = (cols_tiles - 1) * TILE + band_cols
    padded = jnp.pad(padded, ((0, 0), (0, 0), (0, 0), (0, need_cols - pad_cols)))
    width_all = padded.shape[3]
    band_index = jnp.arange(band_rows, dtype=jnp.int32)
    col_index = jnp.arange(band_cols, dtype=jnp.int32)
    inner = jnp.arange(size, dtype=jnp.int32)

    def one_row(group):
        section = group // rows_tiles
        tile_row = group % rows_tiles
        band = lax.dynamic_slice(
            padded,
            index_tuple((section, 0, tile_row * TILE, 0)),
            (1, channels, band_rows, width_all),
        )[0]
        col_bands = jnp.stack(
            [band[:, :, tx * TILE : tx * TILE + band_cols] for tx in range(cols_tiles)], 0
        )
        rows_here = row_starts[group]
        cols_here = col_starts[group]
        pick_rows = (
            band_index[None, None, :] == inner[None, :, None] + rows_here[:, None, None]
        ).astype(jnp.bfloat16)
        picked = jnp.einsum(
            "tip,tcpq->tciq", pick_rows, col_bands, preferred_element_type=jnp.float32
        ).astype(jnp.bfloat16)
        pick_cols = (
            col_index[None, :, None] == inner[None, None, :] + cols_here[:, None, None]
        ).astype(jnp.bfloat16)
        window = jnp.einsum("tciq,tqj->tcij", picked, pick_cols, preferred_element_type=jnp.float32)
        return consume(group, section, tile_row, window)

    return lax.map(one_row, jnp.arange(row_groups, dtype=jnp.int32))


def score_tiles(features, reference_pad, coarse):
    sections, channels, row_count, col_count = features.shape
    rows_tiles = row_count // TILE
    cols_tiles = col_count // TILE
    span_side = 2 * R + 1
    reach_rows = MAXD + R
    row_starts = (coarse[0] + reach_rows - R).reshape(sections * rows_tiles, cols_tiles)
    col_starts = (coarse[1] + reach_rows - R).reshape(sections * rows_tiles, cols_tiles)

    def consume(group, section, tile_row, window):
        strip = lax.dynamic_slice(
            features, index_tuple((section, 0, tile_row * TILE, 0)), (1, channels, TILE, col_count)
        )[0]
        moving = (
            strip.reshape(channels, TILE, cols_tiles, TILE)
            .transpose(2, 0, 1, 3)
            .astype(jnp.float32)
        )
        partials = [
            jnp.sum(moving * window[:, :, i : i + TILE, j : j + TILE], axis=(1, 2, 3))
            for i in range(span_side)
            for j in range(span_side)
        ]
        return jnp.stack(partials, -1)

    result = tile_rows(
        reference_pad, row_starts, col_starts, TILE + 2 * R, TILE + 2 * reach_rows, consume
    )
    return result.reshape(sections, rows_tiles, cols_tiles, span_side * span_side)


def warp_tiles(padded, drift_field, margin, row_count, col_count):
    sections, channels = (padded.shape[0], padded.shape[1])
    rows_tiles = row_count // TILE
    cols_tiles = col_count // TILE
    floor_row = jnp.floor(drift_field[0])
    floor_col = jnp.floor(drift_field[1])
    frac_row = (drift_field[0] - floor_row).reshape(sections * rows_tiles, cols_tiles)
    frac_col = (drift_field[1] - floor_col).reshape(sections * rows_tiles, cols_tiles)
    row_starts = (margin + floor_row.astype(jnp.int32)).reshape(sections * rows_tiles, cols_tiles)
    col_starts = (margin + floor_col.astype(jnp.int32)).reshape(sections * rows_tiles, cols_tiles)

    def consume(group, section, tile_row, window):
        weight_row = frac_row[group][:, None, None, None]
        weight_col = frac_col[group][:, None, None, None]
        upper_mix = (1 - weight_col) * window[:, :, :TILE, :TILE] + weight_col * window[
            :, :, :TILE, 1:
        ]
        lower_mix = (1 - weight_col) * window[:, :, 1:, :TILE] + weight_col * window[:, :, 1:, 1:]
        mixed = ((1 - weight_row) * upper_mix + weight_row * lower_mix).astype(jnp.bfloat16)
        return mixed.transpose(1, 2, 0, 3).reshape(channels, TILE, col_count)

    result = tile_rows(padded, row_starts, col_starts, TILE + 1, TILE + 2 * margin, consume)
    result = result.reshape(sections, rows_tiles, channels, TILE, col_count)
    return result.transpose(0, 2, 1, 3, 4).reshape(sections, channels, row_count, col_count)


def smooth_field(drift_field, counts):
    extended = padded_2(drift_field, (("area", 2),), 1)
    extended = jnp.pad(extended, ((0, 0), (0, 0), (0, 0), (1, 1)))
    neighbours = (
        extended[:, :, :-2, 1:-1]
        + extended[:, :, 2:, 1:-1]
        + extended[:, :, 1:-1, :-2]
        + extended[:, :, 1:-1, 2:]
    )
    return (drift_field + neighbours) / (1.0 + counts)


def local(features, coarse):
    sections, channels, row_count, col_count = features.shape
    margin = (sections * lax.axis_size("sec") - 1) * (MAXD + R) + 1
    reach_rows = MAXD + R
    own_rim = padded_2(features, (("area", 2),), margin)
    prior = shifted(features[-1], "sec", 1)
    reference_core = jnp.concatenate([prior[None], features[:-1]], 0)
    reference_rows = padded_2(reference_core, (("area", 2),), reach_rows)
    reference_pad = jnp.pad(reference_rows, ((0, 0), (0, 0), (0, 0), (reach_rows, reach_rows)))
    partial_scores = score_tiles(features, reference_pad, coarse)
    score_scale = 1.0 / math.sqrt(C * TILE * TILE)
    scores = lax.psum(partial_scores, "chan") * score_scale
    fine = centroid(scores)
    section_index = lax.axis_index("sec") * sections + jnp.arange(sections, dtype=jnp.int32)
    keep = (section_index >= 1).astype(jnp.float32)
    pair_field = (coarse.astype(jnp.float32) + fine) * keep[None, :, None, None]
    local_sum = jnp.cumsum(pair_field, axis=1)
    device_total = local_sum[:, -1]
    earlier = prefix(device_total, "sec", combine_add, jnp.zeros_like(device_total))
    drift_field = local_sum + earlier[:, None]
    rows_tiles = row_count // TILE
    cols_tiles = col_count // TILE
    total_rows = rows_tiles * lax.axis_size("area")
    global_row = lax.axis_index("area") * rows_tiles + jnp.arange(rows_tiles, dtype=jnp.int32)
    local_col = jnp.arange(cols_tiles, dtype=jnp.int32)
    vertical = (global_row > 0).astype(jnp.float32) + (global_row < total_rows - 1).astype(
        jnp.float32
    )
    sideways = (local_col > 0).astype(jnp.float32) + (local_col < cols_tiles - 1).astype(
        jnp.float32
    )
    counts = vertical[:, None] + sideways[None, :]
    for sweep in range(SMOOTH):
        drift_field = smooth_field(drift_field, counts)
    source = jnp.pad(own_rim, ((0, 0), (0, 0), (0, 0), (margin, margin)))
    warped = warp_tiles(source, drift_field, margin, row_count, col_count)
    return (warped, drift_field)


def solution(mesh):
    placed = (P("sec", "chan", "area", None), P(None, "sec", "area", None))
    return jax.shard_map(
        local,
        mesh=mesh,
        in_specs=placed,
        out_specs=(P("sec", "chan", "area", None), P(None, "sec", "area", None)),
        check_vma=False,
    )
```

profile of v0, /device:TPU:197, one launch (start us, length us, event | category | flops | bytes accessed | tf_op | source)
XLA Modules:
  0.0 1035.9 jit_solution(5155870344864464140)
XLA Ops:
  13.9 41.5 %collective-permute-done = bf16[16,256,256]{2,1,0:T(8,128)(2,1)} collective-permute-done((bf16[16,256,256]{2,1,0:T(8,128)(2,1)}, bf16[16,256,256]{2,1,0:T(8,128)(2,1)}, u32[]{:S(2)}, u32[]{:S(2)}) %collective-permute-start) | collective-permute-done | bytes 2097184 | tf_op jit(solution)/shard_map/ppermute | solution.py:35
  56.9 47.2 %collective-permute-start.1 = (bf16[2,16,8,256]{3,2,1,0:T(8,128)(2,1)}, bf16[2,16,8,256]{3,2,1,0:T(8,128)(2,1)S(1)}, u32[]{:S(2)}, u32[]{:S(2)}) collective-permute-start(bf16[2,16,8,256]{3,2,1,0:T(8,128)(2,1)} %get-tuple-element.568), channel_id=1, source_target_pairs={{0,4},{4,8},{8,12},{12,16},{16,20},{20,24},{24,28},{28,32},{32,36}... | collective-permute-start | bytes 393224 | tf_op jit(solution)/shard_map/ppermute | solution.py:23
  111.7 6.8 select_maximum_fusion
  122.0 379.0 %while.42 = (s32[]{:T(128)}, f32[16,8,9]{2,1,0:T(8,128)S(1)}, s32[16]{0:T(128)S(1)}, bf16[2,16,256,256]{3,2,1,0:T(8,128)(2,1)}, bf16[2,16,272,352]{3,2,1,0:T(8,1...) while((s32[]{:T(128)}, f32[16,8,9]{2,1,0:T(8,128)S(1)}, ...), condition=%wide.region_10.11_spmd.clone.clone, body=%wide.region_0.10_spmd.clone.clone.sunk | while | flops 94452984 | bytes 13492694 | solution.py:111
  139.8 5.8 fusion.160
  163.5 5.8 fusion.160
  187.2 5.8 fusion.160
  210.9 5.8 fusion.160
  234.6 5.8 fusion.160
  258.3 5.8 fusion.160
  281.9 5.8 fusion.160
  305.6 5.8 fusion.160
  329.3 5.8 fusion.160
  353.0 5.8 fusion.160
  376.7 5.8 fusion.160
  400.4 5.8 fusion.160
  424.1 5.8 fusion.160
  447.7 5.8 fusion.160
  471.4 5.8 fusion.160
  495.1 5.8 fusion.160
  501.0 14.2 %psum.7 = f32[2,8,8,9]{3,2,1,0:T(8,128)S(1)} all-reduce(f32[2,8,8,9]{3,2,1,0:T(8,128)S(1)} %bitcast.254), channel_id=1, replica_groups=mesh['sec'=4,'area'=16,'chan'=4] {'chan'}, use_global_device_ids=true, to_apply=%region_11.12 | all-reduce | flops 1152 | bytes 9216 | tf_op jit(solution)/shard_map/psum | solution.py:194
  515.4 19.5 %all-gather = f32[8,1,8,8]{3,2,1,0:T(8,128)S(1)} all-gather(f32[2,1,8,8]{3,2,1,0:T(8,128)S(1)} %slice.391), channel_id=2, replica_groups=mesh['sec'=4,'area'=16,'chan'=4] {'sec'}, dimensions={0}, use_global_device_ids=true | all-gather | bytes 2560 | tf_op jit(solution)/shard_map/all_gather | solution.py:40
  535.1 10.7 %collective-permute-start.3 = (f32[2,2,1,8]{3,2,1,0:T(1,128)S(1)}, f32[2,2,1,8]{3,2,1,0:T(1,128)S(1)}, u32[]{:S(2)}, u32[]{:S(2)}) collective-permute-start(f32[2,2,1,8]{3,2,1,0:T(1,128)S(1)} %get-tuple-element.578), channel_id=1, source_target_pairs={{0,4},{4,8},{8,12},{12,16},{16,20},{20,24},{24,28},{28,32},{32,36}... | collective-permute-start | bytes 392 | tf_op jit(solution)/shard_map/ppermute | solution.py:23
  555.4 9.2 fusion.79
  571.0 6.0 pad.32
  577.7 453.3 %while.43 = (s32[]{:T(128)}, bf16[16,16,32,256]{3,2,1,0:T(8,128)(2,1)}, s32[16]{0:T(128)S(1)}, f32[16,8]{1,0:T(8,128)S(1)}, f32[16,8]{1,0:T(8,128)S(1)}, /*index...) while((s32[]{:T(128)}, ...), condition=%wide.region_19.20_spmd.clone.clone, body=%wide.region_18.19_spmd.clone.clone.sunk | while | flops 389619904 | bytes 38078564 | solution.py:111
  710.7 5.1 fusion.174
  767.4 5.1 fusion.174
  795.7 5.1 fusion.174
  880.6 5.1 fusion.174
  909.0 5.1 fusion.174
  965.7 5.1 fusion.174
  (813 shorter events, 626.3 us)
Async XLA Ops:
  4.7 50.7 %collective-permute-start = (bf16[16,256,256]{2,1,0:T(8,128)(2,1)}, bf16[16,256,256]{2,1,0:T(8,128)(2,1)}, u32[]{:S(2)}, u32[]{:S(2)}) collective-permute-start(bf16[16,256,256]{2,1,0:T(8,128)(2,1)} %get-tuple-element.570), channel_id=1, source_target_pairs={{0,64},{64,128},{128,192},{1,65},{65,129},{129,193},{2,66},{66,130... | collective-permute-start | bytes 6291464 | tf_op jit(solution)/shard_map/ppermute | solution.py:35
  7.1 100.9 %collective-permute-start.9 = (bf16[2,16,57,256]{3,1,2,0:T(8,128)(2,1)S(1)}, bf16[2,16,57,256]{3,1,2,0:T(8,128)(2,1)}, u32[]{:S(2)}, u32[]{:S(2)}) collective-permute-start(bf16[2,16,57,256]{3,1,2,0:T(8,128)(2,1)S(1)} %copy.56), channel_id=1, source_target_pairs={{0,4},{4,8},{8,12},{12,16},{16,20},{20,24},{24,28},{28,32},{32,36}... | collective-permute-start | bytes 2801672 | tf_op jit(solution)/shard_map/ppermute | solution.py:23
  11.8 535.8 %collective-permute-start.10 = (bf16[2,16,57,256]{3,1,2,0:T(8,128)(2,1)}, bf16[2,16,57,256]{3,1,2,0:T(8,128)(2,1)}, u32[]{:S(2)}, u32[]{:S(2)}) collective-permute-start(bf16[2,16,57,256]{3,1,2,0:T(8,128)(2,1)} %copy.57), channel_id=1, source_target_pairs={{4,0},{8,4},{12,8},{16,12},{20,16},{24,20},{28,24},{32,28},{36,32}... | collective-permute-start | bytes 2801672 | tf_op jit(solution)/shard_map/ppermute | solution.py:25
  56.9 53.5 %collective-permute-start.1 = (bf16[2,16,8,256]{3,2,1,0:T(8,128)(2,1)}, bf16[2,16,8,256]{3,2,1,0:T(8,128)(2,1)S(1)}, u32[]{:S(2)}, u32[]{:S(2)}) collective-permute-start(bf16[2,16,8,256]{3,2,1,0:T(8,128)(2,1)} %get-tuple-element.568), channel_id=1, source_target_pairs={{0,4},{4,8},{8,12},{12,16},{16,20},{20,24},{24,28},{28,32},{32,36}... | collective-permute-start | bytes 393224 | tf_op jit(solution)/shard_map/ppermute | solution.py:23
  104.1 7.5 collective-permute-start.2
  122.0 393.2 %copy-start.10 = (f32[9]{0:T(128)S(1)}, f32[9]{0:T(128)}, u32[]{:S(2)}) copy-start(f32[9]{0:T(128)} %get-tuple-element.584) | copy-start | bytes 112
  122.0 393.2 %copy-start.11 = (f32[9]{0:T(128)S(1)}, f32[9]{0:T(128)}, u32[]{:S(2)}) copy-start(f32[9]{0:T(128)} %get-tuple-element.585) | copy-start | bytes 112
  122.0 393.3 %copy-start.3 = (s32[2,2,8,8]{3,2,1,0:T(8,128)S(1)}, s32[2,2,8,8]{3,2,1,0:T(8,128)}, u32[]{:S(2)}) copy-start(s32[2,2,8,8]{3,2,1,0:T(8,128)} %param.9) | copy-start | bytes 3076
  122.0 15.0 %copy-start.6 = (s32[16,8]{1,0:T(8,128)}, s32[16,8]{1,0:T(8,128)S(1)}, u32[]{:S(2)}) copy-start(s32[16,8]{1,0:T(8,128)S(1)} %get-tuple-element.781) | copy-start | bytes 1540 | tf_op jit(solution)/shard_map/while
  122.1 15.0 %copy-start.8 = (s32[16,8]{1,0:T(8,128)}, s32[16,8]{1,0:T(8,128)S(1)}, u32[]{:S(2)}) copy-start(s32[16,8]{1,0:T(8,128)S(1)} %get-tuple-element.780) | copy-start | bytes 1540 | tf_op jit(solution)/shard_map/while
  145.7 15.0 %copy-start.8 = (s32[16,8]{1,0:T(8,128)}, s32[16,8]{1,0:T(8,128)S(1)}, u32[]{:S(2)}) copy-start(s32[16,8]{1,0:T(8,128)S(1)} %get-tuple-element.780) | copy-start | bytes 1540 | tf_op jit(solution)/shard_map/while
  169.4 14.9 %copy-start.6 = (s32[16,8]{1,0:T(8,128)}, s32[16,8]{1,0:T(8,128)S(1)}, u32[]{:S(2)}) copy-start(s32[16,8]{1,0:T(8,128)S(1)} %get-tuple-element.781) | copy-start | bytes 1540 | tf_op jit(solution)/shard_map/while
  169.4 15.0 %copy-start.8 = (s32[16,8]{1,0:T(8,128)}, s32[16,8]{1,0:T(8,128)S(1)}, u32[]{:S(2)}) copy-start(s32[16,8]{1,0:T(8,128)S(1)} %get-tuple-element.780) | copy-start | bytes 1540 | tf_op jit(solution)/shard_map/while
  193.1 14.9 %copy-start.6 = (s32[16,8]{1,0:T(8,128)}, s32[16,8]{1,0:T(8,128)S(1)}, u32[]{:S(2)}) copy-start(s32[16,8]{1,0:T(8,128)S(1)} %get-tuple-element.781) | copy-start | bytes 1540 | tf_op jit(solution)/shard_map/while
  193.1 15.0 %copy-start.8 = (s32[16,8]{1,0:T(8,128)}, s32[16,8]{1,0:T(8,128)S(1)}, u32[]{:S(2)}) copy-start(s32[16,8]{1,0:T(8,128)S(1)} %get-tuple-element.780) | copy-start | bytes 1540 | tf_op jit(solution)/shard_map/while
  240.5 14.9 %copy-start.6 = (s32[16,8]{1,0:T(8,128)}, s32[16,8]{1,0:T(8,128)S(1)}, u32[]{:S(2)}) copy-start(s32[16,8]{1,0:T(8,128)S(1)} %get-tuple-element.781) | copy-start | bytes 1540 | tf_op jit(solution)/shard_map/while
  240.5 15.0 %copy-start.8 = (s32[16,8]{1,0:T(8,128)}, s32[16,8]{1,0:T(8,128)S(1)}, u32[]{:S(2)}) copy-start(s32[16,8]{1,0:T(8,128)S(1)} %get-tuple-element.780) | copy-start | bytes 1540 | tf_op jit(solution)/shard_map/while
  287.8 14.9 %copy-start.6 = (s32[16,8]{1,0:T(8,128)}, s32[16,8]{1,0:T(8,128)S(1)}, u32[]{:S(2)}) copy-start(s32[16,8]{1,0:T(8,128)S(1)} %get-tuple-element.781) | copy-start | bytes 1540 | tf_op jit(solution)/shard_map/while
  287.8 15.0 %copy-start.8 = (s32[16,8]{1,0:T(8,128)}, s32[16,8]{1,0:T(8,128)S(1)}, u32[]{:S(2)}) copy-start(s32[16,8]{1,0:T(8,128)S(1)} %get-tuple-element.780) | copy-start | bytes 1540 | tf_op jit(solution)/shard_map/while
  335.2 14.9 %copy-start.6 = (s32[16,8]{1,0:T(8,128)}, s32[16,8]{1,0:T(8,128)S(1)}, u32[]{:S(2)}) copy-start(s32[16,8]{1,0:T(8,128)S(1)} %get-tuple-element.781) | copy-start | bytes 1540 | tf_op jit(solution)/shard_map/while
  335.2 15.0 %copy-start.8 = (s32[16,8]{1,0:T(8,128)}, s32[16,8]{1,0:T(8,128)S(1)}, u32[]{:S(2)}) copy-start(s32[16,8]{1,0:T(8,128)S(1)} %get-tuple-element.780) | copy-start | bytes 1540 | tf_op jit(solution)/shard_map/while
  382.6 15.0 %copy-start.8 = (s32[16,8]{1,0:T(8,128)}, s32[16,8]{1,0:T(8,128)S(1)}, u32[]{:S(2)}) copy-start(s32[16,8]{1,0:T(8,128)S(1)} %get-tuple-element.780) | copy-start | bytes 1540 | tf_op jit(solution)/shard_map/while
  430.0 15.0 %copy-start.8 = (s32[16,8]{1,0:T(8,128)}, s32[16,8]{1,0:T(8,128)S(1)}, u32[]{:S(2)}) copy-start(s32[16,8]{1,0:T(8,128)S(1)} %get-tuple-element.780) | copy-start | bytes 1540 | tf_op jit(solution)/shard_map/while
  477.3 14.9 %copy-start.6 = (s32[16,8]{1,0:T(8,128)}, s32[16,8]{1,0:T(8,128)S(1)}, u32[]{:S(2)}) copy-start(s32[16,8]{1,0:T(8,128)S(1)} %get-tuple-element.781) | copy-start | bytes 1540 | tf_op jit(solution)/shard_map/while
  477.3 15.0 %copy-start.8 = (s32[16,8]{1,0:T(8,128)}, s32[16,8]{1,0:T(8,128)S(1)}, u32[]{:S(2)}) copy-start(s32[16,8]{1,0:T(8,128)S(1)} %get-tuple-element.780) | copy-start | bytes 1540 | tf_op jit(solution)/shard_map/while
  501.0 54.4 %copy-start.1 = (bf16[2,16,57,256]{3,2,1,0:T(8,128)(2,1)S(1)}, bf16[2,16,57,256]{3,2,1,0:T(8,128)(2,1)}, u32[]{:S(2)}) copy-start(bf16[2,16,57,256]{3,2,1,0:T(8,128)(2,1)} %copy.41) | copy-start | bytes 2801668
  535.1 14.1 %collective-permute-start.3 = (f32[2,2,1,8]{3,2,1,0:T(1,128)S(1)}, f32[2,2,1,8]{3,2,1,0:T(1,128)S(1)}, u32[]{:S(2)}, u32[]{:S(2)}) collective-permute-start(f32[2,2,1,8]{3,2,1,0:T(1,128)S(1)} %get-tuple-element.578), channel_id=1, source_target_pairs={{0,4},{4,8},{8,12},{12,16},{16,20},{20,24},{24,28},{28,32},{32,36}... | collective-permute-start | bytes 392 | tf_op jit(solution)/shard_map/ppermute | solution.py:23
  545.8 4.9 collective-permute-start.4
  550.8 13.7 %collective-permute-start.5 = (f32[2,2,1,8]{3,2,1,0:T(1,128)S(1)}, f32[2,2,1,8]{3,2,1,0:T(1,128)S(1)}, u32[]{:S(2)}, u32[]{:S(2)}) collective-permute-start(f32[2,2,1,8]{3,2,1,0:T(1,128)S(1)} %get-tuple-element.576), channel_id=1, source_target_pairs={{0,4},{4,8},{8,12},{12,16},{16,20},{20,24},{24,28},{28,32},{32,36}... | collective-permute-start | bytes 392 | tf_op jit(solution)/shard_map/ppermute | solution.py:23
  553.1 11.5 %collective-permute-start.6 = (f32[2,2,1,8]{3,2,1,0:T(1,128)S(1)}, f32[2,2,1,8]{3,2,1,0:T(1,128)S(1)}, u32[]{:S(2)}, u32[]{:S(2)}) collective-permute-start(f32[2,2,1,8]{3,2,1,0:T(1,128)S(1)} %get-tuple-element.577), channel_id=1, source_target_pairs={{4,0},{8,4},{12,8},{16,12},{20,16},{24,20},{28,24},{32,28},{36,32}... | collective-permute-start | bytes 392 | tf_op jit(solution)/shard_map/ppermute | solution.py:25
  564.8 12.2 %collective-permute-start.7 = (f32[2,2,1,8]{3,2,1,0:T(1,128)S(1)}, f32[2,2,1,8]{3,2,1,0:T(1,128)S(1)}, u32[]{:S(2)}, u32[]{:S(2)}) collective-permute-start(f32[2,2,1,8]{3,2,1,0:T(1,128)S(1)} %get-tuple-element.574), channel_id=1, source_target_pairs={{0,4},{4,8},{8,12},{12,16},{16,20},{20,24},{24,28},{28,32},{32,36}... | collective-permute-start | bytes 392 | tf_op jit(solution)/shard_map/ppermute | solution.py:23
  568.5 8.5 collective-permute-start.8
  (51 other events, 429.7 us)
where the time goes:
time: 1050 us; the launch traced here: 1040 us
  local copies, waits for them, and re-layouts  467 us (44%)
  other arithmetic  155 us (15%)
  loops' own time  131 us (12%)
  matrix products  124 us (12%)
  starting transfers between devices  80.1 us (8%)
  waiting for transfers between devices  44.2 us (4%)
  blocking collectives  33.7 us (3%)
    while x352, local copies, waits for them, and re-layouts  255 us
    another operation x2, loops' own time, tile_rows(): return lax.map(one_row, jnp.arange(row_groups, dtype=jnp.int32))  131 us
    dot_general x32, matrix products, one_row(): jnp.einsum('tciq,tqj->tcij', picked, pick_cols, preferred_element_type=jn...  124 us
    reduce_sum x16, other arithmetic, consume(): jnp.sum(moving * window[:, :, i:i + TILE, j:j + TILE], axis=(1, 2, 3))  92.2 us
    ppermute x5, starting transfers between devices, padded_2(): lax.ppermute(tail, axis, [(i, (i + 1) % count) for i in range(ends)])  67 us
    squeeze x32, local copies, waits for them, and re-layouts, one_row(): lax.dynamic_slice(padded, index_tuple((section, 0, tile_row * TILE, 0)),...  62.9 us
    ppermute x1, waiting for transfers between devices, shifted(): return lax.ppermute(shard, axis, pairs)  41.5 us
    another operation x32, local copies, waits for them, and re-layouts, one_row(): jnp.stack([band[:, :, tx * TILE:tx * TILE + band_cols] for tx in range(co...  38.9 us
  transfers between devices with their start and end apart: 11, of which 3 were waited for; matrix products, arithmetic and copies ran while one was open for 33% of the time, Pallas kernels for 0%

commit v1 on v0

v1 whole, which is shorter than its diff:
```python
import math

import jax
import jax.numpy as jnp
from jax import lax
from jax.experimental import pallas as pl
from jax.experimental.pallas import tpu as pltpu

from jax.sharding import PartitionSpec as P

C = 64
TILE = 32
MAXD = 7
R = 1
SMOOTH = 3
HALO = 64
BF = jnp.bfloat16
F32 = jnp.float32


def lane_pick(scalars, lanes_tile):
    out = jnp.full(lanes_tile.shape, scalars[0])
    for t in range(1, len(scalars)):
        out = jnp.where(lanes_tile == t, scalars[t], out)
    return out


def score_row(f_rows, p_rows, coarse_row, coarse_col, left, right, count):
    src = lax.broadcasted_iota(jnp.int32, (256, 128), 0)
    lane = lax.broadcasted_iota(jnp.int32, (1, 128), 1)
    lane_tile = lane // TILE
    shifts = []
    for h in range(2):
        col = lane + 128 * h + lane_pick([coarse_col[4 * h + t] for t in range(4)], lane_tile)
        rel = src - col
        for b in (-1, 0, 1):
            shifts.append(jnp.where(rel == b, 1.0, 0.0).astype(BF))
    shifted = jnp.concatenate(shifts, 1)
    window = p_rows()
    for c0 in range(0, count, 4):
        moved = lax.dot_general(
            window[c0 * 64 : (c0 + 4) * 64], shifted, (((1,), (0,)), ((), ())), preferred_element_type=F32
        ).astype(BF)
        for c in range(c0, c0 + 4):
            for h in range(2):
                for b in range(3):
                    right[h, 64 * b : 64 * b + 64, 128 * c : 128 * c + 128] = moved[
                        64 * (c - c0) : 64 * (c - c0) + 64, 384 * h + 128 * b : 384 * h + 128 * b + 128
                    ]
    tile_masks = [lax.broadcasted_iota(jnp.int32, (TILE, 128), 1) // TILE == t for t in range(4)]
    for c in range(count):
        strip = f_rows(c)
        for h in range(2):
            part = strip[:, 128 * h : 128 * h + 128]
            for t in range(4):
                left[h, TILE * t : TILE * t + TILE, 128 * c : 128 * c + 128] = jnp.where(
                    tile_masks[t], part, jnp.zeros_like(part)
                )
    row = lax.broadcasted_iota(jnp.int32, (128, 192), 0)
    col = lax.broadcasted_iota(jnp.int32, (128, 192), 1)
    base = col % 64 - 16 - row % TILE
    row_tile = lax.broadcasted_iota(jnp.int32, (128, 1), 0) // TILE
    out = [[], [], []]
    for h in range(2):
        gram = lax.dot_general(
            left[h, :, : count * 128],
            right[h, :, : count * 128],
            (((1,), (1,)), ((), ())),
            preferred_element_type=F32,
        )
        rel = base - lane_pick([coarse_row[4 * h + t] for t in range(4)], row_tile)
        for a in range(3):
            kept = jnp.where(rel == a - 1, gram, 0.0)
            out[a].append(jnp.sum(kept.reshape(4, TILE, 192), axis=1))
    return [jnp.concatenate(o, 0) for o in out]


def score_kernel(coarse, f_ref, p0_ref, p1_ref, out_ref, left, right, acc):
    for s, p_ref in ((0, p0_ref), (1, p1_ref)):

        def step(ty, _):
            crow = [coarse[0, s * 64 + ty * 8 + t] for t in range(8)]
            ccol = [coarse[1, s * 64 + ty * 8 + t] for t in range(8)]
            top = pl.multiple_of(ty * TILE, TILE)
            blocks = score_row(
                lambda c: f_ref[s, c, pl.ds(top, TILE), :],
                lambda: p_ref[:, pl.ds(top, 64), :].reshape(16 * 64, 256),
                crow,
                ccol,
                left,
                right,
                16,
            )
            for a in range(3):
                acc[a, pl.ds(pl.multiple_of(s * 64 + ty * 8, 8), 8), :] = blocks[a]
            return 0

        lax.fori_loop(0, 8, step, 0)
    seg = lax.broadcasted_iota(jnp.int32, (8, 192), 1) // 64
    pick = (seg == lax.broadcasted_iota(jnp.int32, (8, 192), 0)).astype(F32)
    for a in range(3):
        out_ref[a] = lax.dot_general(
            pick, acc[a], (((1,), (1,)), ((), ())), precision=lax.Precision.HIGHEST, preferred_element_type=F32
        )


def scores_local(coarse, features, prior0, prior1):
    vm = pl.BlockSpec(memory_space=pltpu.VMEM)
    return pl.pallas_call(
        score_kernel,
        out_shape=jax.ShapeDtypeStruct((3, 8, 128), F32),
        in_specs=[pl.BlockSpec(memory_space=pltpu.SMEM), vm, vm, vm],
        out_specs=vm,
        scratch_shapes=[
            pltpu.VMEM((2, 128, 2048), BF),
            pltpu.VMEM((2, 192, 2048), BF),
            pltpu.VMEM((3, 128, 192), F32),
        ],
        compiler_params=pltpu.CompilerParams(vmem_limit_bytes=56 * 2**20),
        name="scores",
    )(coarse, features, prior0, prior1)


def warp_kernel(whole, frac, src, out_ref, held, rows, sems):
    step = pl.program_id(0)
    s = step // 8
    ty = step % 8

    def load(k):
        return pltpu.make_async_copy(src.at[k], held.at[k], sems.at[k])

    @pl.when(step == 0)
    def _():
        load(0).start()
        load(1).start()
        load(0).wait()

    @pl.when(step == 8)
    def _():
        load(1).wait()

    lane = lax.broadcasted_iota(jnp.int32, (1, 128), 1)
    lane_tile = lane // TILE
    src_col = lax.broadcasted_iota(jnp.int32, (256, 128), 0)
    base = HALO + TILE * ty
    for h in range(2):
        at = step * 8 + 4 * h
        fl_row = [whole[0, at + t] for t in range(4)]
        fl_col = [whole[1, at + t] for t in range(4)]
        fr_row = lane_pick([frac[0, at + t] for t in range(4)], lane_tile)
        fr_col = lane_pick([frac[1, at + t] for t in range(4)], lane_tile)
        low = jnp.minimum(jnp.minimum(fl_row[0], fl_row[1]), jnp.minimum(fl_row[2], fl_row[3]))
        high = jnp.maximum(jnp.maximum(fl_row[0], fl_row[1]), jnp.maximum(fl_row[2], fl_row[3]))
        start = jnp.minimum((base + low) // 16 * 16, 2 * HALO + 256 - 48)
        chunks = (base + high + TILE + 1 - start + 15) // 16
        rel = src_col - (lane + 128 * h + lane_pick(fl_col, lane_tile))
        weight = jnp.where(rel == 0, 1.0 - fr_col, jnp.where(rel == 1, fr_col, 0.0))
        coarse_part = weight.astype(BF)
        fine_part = (weight - coarse_part.astype(F32)).astype(BF)
        mixer = jnp.concatenate([coarse_part, fine_part], 1)

        def chunk(r, _):
            at_row = pl.multiple_of(start + 16 * r, 16)
            block = held[s, :, pl.ds(at_row, 16), :].reshape(256, 256)
            mixed = jnp.dot(block, mixer, preferred_element_type=F32)
            mixed = mixed[:, :128] + mixed[:, 128:]
            rows[:, pl.ds(pl.multiple_of(16 * r, 16), 16), :] = mixed.reshape(16, 16, 128)
            return 0

        for r in range(3):
            chunk(r, 0)
        lax.fori_loop(3, chunks, chunk, 0)
        offs = [base + fl_row[t] - start for t in range(4)]
        for c in range(16):
            upper = rows[c, pl.ds(offs[0], TILE), :]
            lower = rows[c, pl.ds(offs[0] + 1, TILE), :]
            for t in range(1, 4):
                mine = lane_tile == t
                upper = jnp.where(mine, rows[c, pl.ds(offs[t], TILE), :], upper)
                lower = jnp.where(mine, rows[c, pl.ds(offs[t] + 1, TILE), :], lower)
            out_ref[0, c, :, 128 * h : 128 * h + 128] = ((1.0 - fr_row) * upper + fr_row * lower).astype(BF)


def warp_local(whole, frac, source):
    sm = pl.BlockSpec(memory_space=pltpu.SMEM)
    return pl.pallas_call(
        warp_kernel,
        grid=(16,),
        out_shape=jax.ShapeDtypeStruct((2, 16, 256, 256), BF),
        in_specs=[sm, sm, pl.BlockSpec(memory_space=pl.ANY)],
        out_specs=pl.BlockSpec((1, 16, TILE, 256), lambda g: (g // 8, 0, g % 8, 0)),
        scratch_shapes=[
            pltpu.VMEM((2, 16, 2 * HALO + 256, 256), BF),
            pltpu.VMEM((16, 176, 128), F32),
            pltpu.SemaphoreType.DMA((2,)),
        ],
        compiler_params=pltpu.CompilerParams(vmem_limit_bytes=56 * 2**20),
        name="warp",
    )(whole, frac, source)


def padded_2(cells, sides, width):
    for axis, dim in sides:
        count = lax.axis_size(axis)
        ends = count - 1
        head = lax.slice_in_dim(cells, 0, width, axis=dim)
        tail = lax.slice_in_dim(cells, cells.shape[dim] - width, cells.shape[dim], axis=dim)
        cells = jnp.concatenate(
            [
                lax.ppermute(tail, axis, [(i, (i + 1) % count) for i in range(ends)]),
                cells,
                lax.ppermute(head, axis, [((i + 1) % count, i) for i in range(ends)]),
            ],
            axis=dim,
        )
    return cells


def shifted(shard, axis, by):
    devices = lax.axis_size(axis)
    pairs = [(i, i + by) for i in range(devices) if 0 <= i + by < devices]
    return lax.ppermute(shard, axis, pairs)


def prefix(value, axis, join, neutral):
    count, mine = (lax.axis_size(axis), lax.axis_index(axis))
    pieces = lax.all_gather(value, axis)
    total = jnp.full_like(value, 0) + jnp.asarray(neutral, value.dtype)

    def step(position, total):
        longer = join(total, pieces[position])
        return jnp.where(position < mine, longer, total)

    return lax.fori_loop(0, count - 1, step, total)


def index_tuple(values):
    return tuple((jnp.asarray(value).astype(jnp.int32) for value in values))


def combine_add(earlier, later):
    return earlier + later


def centroid(scores):
    span_side = 2 * R + 1
    offsets = jnp.arange(span_side * span_side, dtype=jnp.int32)
    row_offset = (offsets // span_side - R).astype(jnp.float32)
    col_offset = (offsets % span_side - R).astype(jnp.float32)
    weights = jax.nn.sigmoid(scores)
    weight_total = jnp.sum(weights, axis=-1)
    return jnp.stack(
        [
            jnp.sum(weights * row_offset, axis=-1) / weight_total,
            jnp.sum(weights * col_offset, axis=-1) / weight_total,
        ],
        0,
    )


def smooth_field(drift_field, counts):
    extended = padded_2(drift_field, (("area", 2),), 1)
    extended = jnp.pad(extended, ((0, 0), (0, 0), (0, 0), (1, 1)))
    neighbours = (
        extended[:, :, :-2, 1:-1]
        + extended[:, :, 2:, 1:-1]
        + extended[:, :, 1:-1, :-2]
        + extended[:, :, 1:-1, 2:]
    )
    return (drift_field + neighbours) / (1.0 + counts)


def local(features, coarse):
    sections, channels, row_count, col_count = features.shape
    own = padded_2(features, (("area", 2),), HALO)
    prior = shifted(own[1, :, HALO - 16 : HALO + 272], "sec", 1)
    flat_coarse = coarse.reshape(2, 128)
    sums = scores_local(flat_coarse, features, prior, own[0, :, HALO - 16 : HALO + 272])
    partial_scores = sums[:, :3].reshape(9, 2, 8, 8).transpose(1, 2, 3, 0)
    score_scale = 1.0 / math.sqrt(C * TILE * TILE)
    scores = lax.psum(partial_scores, "chan") * score_scale
    fine = centroid(scores)
    section_index = lax.axis_index("sec") * sections + jnp.arange(sections, dtype=jnp.int32)
    keep = (section_index >= 1).astype(jnp.float32)
    pair_field = (coarse.astype(jnp.float32) + fine) * keep[None, :, None, None]
    local_sum = jnp.cumsum(pair_field, axis=1)
    device_total = local_sum[:, -1]
    earlier = prefix(device_total, "sec", combine_add, jnp.zeros_like(device_total))
    drift_field = local_sum + earlier[:, None]
    rows_tiles = row_count // TILE
    cols_tiles = col_count // TILE
    total_rows = rows_tiles * lax.axis_size("area")
    global_row = lax.axis_index("area") * rows_tiles + jnp.arange(rows_tiles, dtype=jnp.int32)
    local_col = jnp.arange(cols_tiles, dtype=jnp.int32)
    vertical = (global_row > 0).astype(jnp.float32) + (global_row < total_rows - 1).astype(
        jnp.float32
    )
    sideways = (local_col > 0).astype(jnp.float32) + (local_col < cols_tiles - 1).astype(
        jnp.float32
    )
    counts = vertical[:, None] + sideways[None, :]
    for sweep in range(SMOOTH):
        drift_field = smooth_field(drift_field, counts)
    floors = jnp.floor(drift_field)
    warped = warp_local(
        floors.astype(jnp.int32).reshape(2, 128), (drift_field - floors).reshape(2, 128), own
    )
    return (warped, drift_field)


def solution(mesh):
    placed = (P("sec", "chan", "area", None), P(None, "sec", "area", None))
    return jax.shard_map(
        local,
        mesh=mesh,
        in_specs=placed,
        out_specs=(P("sec", "chan", "area", None), P(None, "sec", "area", None)),
        check_vma=False,
    )
```

time: 1050 us -> 253 us (0.24); the launches traced: 1040 us -> 252 us
  local copies, waits for them, and re-layouts: 467 us -> 12.1 us
  other arithmetic: 155 us -> 0.79 us
  loops' own time: 131 us -> 0.03 us
  matrix products: 124 us -> 0 us
  Pallas kernels: 0 us -> 53 us
  starting transfers between devices: 80.1 us -> 28.1 us
  waiting for transfers between devices: 44.2 us -> 84.3 us
  blocking collectives: 33.7 us -> 73.3 us
    while x352 -> x0, local copies, waits for them, and re-layouts: 255 us -> none
    another operation x2 -> x0, loops' own time: 131 us -> none  [tile_rows(): return lax.map(one_row, jnp.arange(row_groups, dtype=jnp.int32))]
    dot_general x32 -> x0, matrix products: 124 us -> none  [one_row(): jnp.einsum('tciq,tqj->tcij', picked, pick_cols, preferred_element_type=jn...]
    reduce_sum x16 -> x0, other arithmetic: 92.2 us -> none  [consume(): jnp.sum(moving * window[:, :, i:i + TILE, j:j + TILE], axis=(1, 2, 3))]
    squeeze x36 -> x1, local copies, waits for them, and re-layouts: 67.1 us -> 2.65 us  [local(): own[0, :, HALO - 16:HALO + 272]]
    pallas_call x0 -> x2, Pallas kernels: none -> 53 us  [the longest x1 28.6 us: warp_local(): pl.pallas_call(warp_kernel, grid=(16,), out_shape=jax.ShapeDtypeStruct((2...]
    ppermute x5 -> x4, starting transfers between devices: 67 us -> 18.2 us  [padded_2(): lax.ppermute(tail, axis, [(i, (i + 1) % count) for i in range(ends)])]
    another operation x64 -> x0, local copies, waits for them, and re-layouts: 40.9 us -> none  [the longest x32 38.9 us: one_row(): jnp.stack([band[:, :, tx * TILE:tx * TILE + band_cols] for tx in range(co...]
  transfers between devices with their start and end apart: 11 -> 9, of which waited for: 3 -> 6; matrix products, arithmetic and copies ran while one was open for 33% -> 1% of each run, Pallas kernels for 0% -> 0%
where the time goes in v1:
time: 253 us; the launch traced here: 252 us
  waiting for transfers between devices  84.3 us (33%)
  blocking collectives  73.3 us (29%)
  Pallas kernels  53 us (21%)
  starting transfers between devices  28.1 us (11%)
  local copies, waits for them, and re-layouts  12.1 us (5%)
    all_gather x1, blocking collectives, prefix(): pieces = lax.all_gather(value, axis)  59 us
    ppermute x1, waiting for transfers between devices, shifted(): return lax.ppermute(shard, axis, pairs)  54.1 us
    pallas_call x1, Pallas kernels, warp_local(): pl.pallas_call(warp_kernel, grid=(16,), out_shape=jax.ShapeDtypeStruct((2...  28.6 us
    pallas_call x1, Pallas kernels, scores_local(): pl.pallas_call(score_kernel, out_shape=jax.ShapeDtypeStruct((3, 8, 128),...  24.4 us
    ppermute x4, starting transfers between devices, padded_2(): lax.ppermute(tail, axis, [(i, (i + 1) % count) for i in range(ends)])  18.2 us
    ppermute x4, waiting for transfers between devices, padded_2(): lax.ppermute(tail, axis, [(i, (i + 1) % count) for i in range(ends)])  16.9 us
    psum x1, blocking collectives, local(): scores = lax.psum(partial_scores, 'chan') * score_scale  14.3 us
    ppermute x4, waiting for transfers between devices, padded_2(): lax.ppermute(head, axis, [((i + 1) % count, i) for i in range(ends)])  13.4 us
  transfers between devices with their start and end apart: 9, of which 6 were waited for; matrix products, arithmetic and copies ran while one was open for 1% of the time, Pallas kernels for 0%

profile of v1, /device:TPU:197, one launch (start us, length us, event | category | flops | bytes accessed | tf_op | source)
XLA Modules:
  0.0 252.4 jit_solution(3716239514044020048)
XLA Ops:
  0.6 1.8 fusion.26
  2.5 3.3 %collective-permute-start = (bf16[2,16,64,256]{3,2,1,0:T(8,128)(2,1)S(1)}, bf16[2,16,64,256]{3,2,1,0:T(8,128)(2,1)S(1)}, u32[]{:S(2)}, u32[]{:S(2)}) collective-permute-start(bf16[2,16,64,256]{3,2,1,0:T(8,128)(2,1)S(1)} %get-tuple-element.113), channel_id=1, source_target_pairs={{0,4},{4,8},{8,12},{12,16},{16,20},{20,24},{24,28},{28,32},{32,36}... | collective-permute-start | bytes 3145736 | tf_op jit(solution)/shard_map/ppermute | solution.py:210
  5.8 1.9 collective-permute-start.1
  7.8 16.8 %collective-permute-done = bf16[2,16,64,256]{3,2,1,0:T(8,128)(2,1)S(1)} collective-permute-done((bf16[2,16,64,256]{3,2,1,0:T(8,128)(2,1)S(1)}, bf16[2,16,64,256]{3,2,1,0:T(8,128)(2,1)S(1)}, u32[]{:S(2)}, u32[]{:S(2)}) %collective-permute-start) | collective-permute-done | bytes 1048608 | tf_op jit(solution)/shard_map/ppermute | solution.py:210
  24.7 0.4 constant_dynamic-update-slice_fusion.1
  25.1 5.4 %collective-permute-done.1 = bf16[2,16,64,256]{3,2,1,0:T(8,128)(2,1)S(1)} collective-permute-done((bf16[2,16,64,256]{3,2,1,0:T(8,128)(2,1)S(1)}, bf16[2,16,64,256]{3,2,1,0:T(8,128)(2,1)S(1)}, u32[]{:S(2)}, u32[]{:S(2)}) %collective-permute-start.1) | collective-permute-done | bytes 1048608 | tf_op jit(solution)/shard_map/ppermute | solution.py:212
  30.6 0.1 constant_dynamic-update-slice_fusion.src
  30.7 2.7 %copy-done.1 = bf16[2,16,384,256]{3,2,1,0:T(8,128)(2,1)} copy-done((bf16[2,16,384,256]{3,2,1,0:T(8,128)(2,1)}, bf16[2,16,384,256]{3,2,1,0:T(8,128)(2,1)S(1)}, u32[]{:S(2)}) %copy-start.1) | copy-done | bytes 6291480
  33.4 2.6 %slice_bitcast_fusion = (bf16[16,288,256]{2,1,0:T(8,128)(2,1)}, bf16[16,288,256]{2,1,0:T(8,128)(2,1)}) fusion(bf16[2,16,384,256]{3,2,1,0:T(8,128)(2,1)S(1)} %constant_dynamic-update-slice_fusion.src), kind=kLoop, calls=%fused_computation.1 | loop fusion | bytes 9437184 | tf_op jit(solution)/shard_map/squeeze | solution.py:278
  36.0 1.3 collective-permute-start.2
  37.3 0.7 reshape.116.coarse
  38.0 54.1 %collective-permute-done.2.p0_ref = bf16[16,288,256]{2,1,0:T(8,128)(2,1)S(1)} collective-permute-done((bf16[16,288,256]{2,1,0:T(8,128)(2,1)}, bf16[16,288,256]{2,1,0:T(8,128)(2,1)S(1)}, u32[]{:S(2)}, u32[]{:S(2)}) %collective-permute-start.2) | collective-permute-done | bytes 2359328 | tf_op jit(solution)/shard_map/ppermute | solution.py:222
  92.1 1.5 copy-done.2
  93.6 24.4 %scores.1 = f32[3,8,128]{2,1,0:T(8,128)} custom-call(s32[2,128]{1,0:T(2,128)} %reshape.116.coarse, bf16[2,16,256,256]{3,2,1,0:T(8,128)(2,1)} %f_ref.1, bf16[16,288,256]{2,1,0:T(8,128)(2,1)} %copy-done.2, bf16[16,288,256]{2,1,0:T(8,128)(2,1)} %get-tuple-element.110.p1_ref), custom_call_target="tpu_custom_call" | custom-call | tf_op jit(solution)/shard_map/scores/pallas_call | solution.py:109
  118.0 0.7 slice.110
  118.7 0.1 reshape.117
  118.8 14.3 %psum.7 = f32[2,8,8,9]{2,1,0,3:T(8,128)S(1)} all-reduce(f32[2,8,8,9]{2,1,0,3:T(8,128)S(1)} %bitcast.20), channel_id=1, replica_groups=mesh['sec'=4,'area'=16,'chan'=4] {'chan'}, use_global_device_ids=true, to_apply=%region_0.0 | all-reduce | flops 1152 | bytes 9216 | tf_op jit(solution)/shard_map/psum | solution.py:281
  133.1 0.1 multiply_reduce_fusion.1
  133.3 59.0 %all-gather = f32[8,1,8,8]{3,2,1,0:T(8,128)S(1)} all-gather(f32[2,1,8,8]{3,2,1,0:T(8,128)S(1)} %slice.111), channel_id=2, replica_groups=mesh['sec'=4,'area'=16,'chan'=4] {'sec'}, dimensions={0}, use_global_device_ids=true | all-gather | bytes 2560 | tf_op jit(solution)/shard_map/all_gather | solution.py:227
  192.4 11.0 %collective-permute-start.3 = (f32[2,2,1,8]{3,2,1,0:T(1,128)S(1)}, f32[2,2,1,8]{3,2,1,0:T(1,128)S(1)}, u32[]{:S(2)}, u32[]{:S(2)}) collective-permute-start(f32[2,2,1,8]{3,2,1,0:T(1,128)S(1)} %get-tuple-element.118), channel_id=1, source_target_pairs={{0,4},{4,8},{8,12},{12,16},{16,20},{20,24},{24,28},{28,32},{32,36}... | collective-permute-start | bytes 392 | tf_op jit(solution)/shard_map/ppermute | solution.py:210
  203.3 1.9 collective-permute-start.4
  205.3 2.9 %collective-permute-done.4 = f32[2,2,1,8]{3,2,1,0:T(1,128)S(1)} collective-permute-done((f32[2,2,1,8]{3,2,1,0:T(1,128)S(1)}, f32[2,2,1,8]{3,2,1,0:T(1,128)S(1)}, u32[]{:S(2)}, u32[]{:S(2)}) %collective-permute-start.4) | collective-permute-done | bytes 160 | tf_op jit(solution)/shard_map/ppermute | solution.py:212
  208.4 2.0 collective-permute-start.5
  210.4 2.4 collective-permute-start.6
  212.8 2.5 collective-permute-done.6
  215.3 0.1 select_maximum_fusion.2
  215.5 2.0 collective-permute-start.7
  217.4 2.4 collective-permute-start.8
  219.8 2.5 collective-permute-done.8
  222.5 0.6 reshape.118.whole
  223.1 0.7 reshape.119.frac
  223.8 28.6 %warp.1 = bf16[2,16,256,256]{3,2,1,0:T(8,128)(2,1)} custom-call(s32[2,128]{1,0:T(2,128)} %reshape.118.whole, f32[2,128]{1,0:T(2,128)} %reshape.119.frac, bf16[2,16,384,256]{3,2,1,0:T(8,128)(2,1)} %copy-done.1), custom_call_target="tpu_custom_call" | custom-call | tf_op jit(solution)/shard_map/warp/pallas_call | solution.py:186
  (34 shorter events, 0.8 us)
Async XLA Ops:
  0.6 24.0 %copy-start = (bf16[2,16,256,256]{3,2,1,0:T(8,128)(2,1)S(1)}, bf16[2,16,256,256]{3,2,1,0:T(8,128)(2,1)}, u32[]{:S(2)}) copy-start(bf16[2,16,256,256]{3,2,1,0:T(8,128)(2,1)} %f_ref.1) | copy-start | bytes 12582916
  2.5 22.1 %collective-permute-start = (bf16[2,16,64,256]{3,2,1,0:T(8,128)(2,1)S(1)}, bf16[2,16,64,256]{3,2,1,0:T(8,128)(2,1)S(1)}, u32[]{:S(2)}, u32[]{:S(2)}) collective-permute-start(bf16[2,16,64,256]{3,2,1,0:T(8,128)(2,1)S(1)} %get-tuple-element.113), channel_id=1, source_target_pairs={{0,4},{4,8},{8,12},{12,16},{16,20},{20,24},{24,28},{28,32},{32,36}... | collective-permute-start | bytes 3145736 | tf_op jit(solution)/shard_map/ppermute | solution.py:210
  5.8 24.8 %collective-permute-start.1 = (bf16[2,16,64,256]{3,2,1,0:T(8,128)(2,1)S(1)}, bf16[2,16,64,256]{3,2,1,0:T(8,128)(2,1)S(1)}, u32[]{:S(2)}, u32[]{:S(2)}) collective-permute-start(bf16[2,16,64,256]{3,2,1,0:T(8,128)(2,1)S(1)} %get-tuple-element.112), channel_id=1, source_target_pairs={{4,0},{8,4},{12,8},{16,12},{20,16},{24,20},{28,24},{32,28},{36,32}... | collective-permute-start | bytes 3145736 | tf_op jit(solution)/shard_map/ppermute | solution.py:212
  25.1 12.2 %copy-start.3 = (s32[2,2,8,8]{3,2,1,0:T(8,128)S(1)}, s32[2,2,8,8]{3,2,1,0:T(8,128)}, u32[]{:S(2)}) copy-start(s32[2,2,8,8]{3,2,1,0:T(8,128)} %param.5) | copy-start | bytes 3076
  30.7 2.7 %copy-start.1 = (bf16[2,16,384,256]{3,2,1,0:T(8,128)(2,1)}, bf16[2,16,384,256]{3,2,1,0:T(8,128)(2,1)S(1)}, u32[]{:S(2)}) copy-start(bf16[2,16,384,256]{3,2,1,0:T(8,128)(2,1)S(1)} %constant_dynamic-update-slice_fusion.src) | copy-start | bytes 18874372
  36.0 56.1 %collective-permute-start.2 = (bf16[16,288,256]{2,1,0:T(8,128)(2,1)}, bf16[16,288,256]{2,1,0:T(8,128)(2,1)S(1)}, u32[]{:S(2)}, u32[]{:S(2)}) collective-permute-start(bf16[16,288,256]{2,1,0:T(8,128)(2,1)} %get-tuple-element.111), channel_id=1, source_target_pairs={{0,64},{64,128},{128,192},{1,65},{65,129},{129,193},{2,66},{66,130... | collective-permute-start | bytes 7077896 | tf_op jit(solution)/shard_map/ppermute | solution.py:222
  92.1 1.5 copy-start.2
  192.4 13.0 %collective-permute-start.3 = (f32[2,2,1,8]{3,2,1,0:T(1,128)S(1)}, f32[2,2,1,8]{3,2,1,0:T(1,128)S(1)}, u32[]{:S(2)}, u32[]{:S(2)}) collective-permute-start(f32[2,2,1,8]{3,2,1,0:T(1,128)S(1)} %get-tuple-element.118), channel_id=1, source_target_pairs={{0,4},{4,8},{8,12},{12,16},{16,20},{20,24},{24,28},{28,32},{32,36}... | collective-permute-start | bytes 392 | tf_op jit(solution)/shard_map/ppermute | solution.py:210
  203.3 4.9 %collective-permute-start.4 = (f32[2,2,1,8]{3,2,1,0:T(1,128)S(1)}, f32[2,2,1,8]{3,2,1,0:T(1,128)S(1)}, u32[]{:S(2)}, u32[]{:S(2)}) collective-permute-start(f32[2,2,1,8]{3,2,1,0:T(1,128)S(1)} %get-tuple-element.119), channel_id=1, source_target_pairs={{4,0},{8,4},{12,8},{16,12},{20,16},{24,20},{28,24},{32,28},{36,32}... | collective-permute-start | bytes 392 | tf_op jit(solution)/shard_map/ppermute | solution.py:212
  208.4 4.3 %collective-permute-start.5 = (f32[2,2,1,8]{3,2,1,0:T(1,128)S(1)}, f32[2,2,1,8]{3,2,1,0:T(1,128)S(1)}, u32[]{:S(2)}, u32[]{:S(2)}) collective-permute-start(f32[2,2,1,8]{3,2,1,0:T(1,128)S(1)} %get-tuple-element.116), channel_id=1, source_target_pairs={{0,4},{4,8},{8,12},{12,16},{16,20},{20,24},{24,28},{28,32},{32,36}... | collective-permute-start | bytes 392 | tf_op jit(solution)/shard_map/ppermute | solution.py:210
  210.4 4.9 %collective-permute-start.6 = (f32[2,2,1,8]{3,2,1,0:T(1,128)S(1)}, f32[2,2,1,8]{3,2,1,0:T(1,128)S(1)}, u32[]{:S(2)}, u32[]{:S(2)}) collective-permute-start(f32[2,2,1,8]{3,2,1,0:T(1,128)S(1)} %get-tuple-element.117), channel_id=1, source_target_pairs={{4,0},{8,4},{12,8},{16,12},{20,16},{24,20},{28,24},{32,28},{36,32}... | collective-permute-start | bytes 392 | tf_op jit(solution)/shard_map/ppermute | solution.py:212
  215.5 4.3 %collective-permute-start.7 = (f32[2,2,1,8]{3,2,1,0:T(1,128)S(1)}, f32[2,2,1,8]{3,2,1,0:T(1,128)S(1)}, u32[]{:S(2)}, u32[]{:S(2)}) collective-permute-start(f32[2,2,1,8]{3,2,1,0:T(1,128)S(1)} %get-tuple-element.114), channel_id=1, source_target_pairs={{0,4},{4,8},{8,12},{12,16},{16,20},{20,24},{24,28},{28,32},{32,36}... | collective-permute-start | bytes 392 | tf_op jit(solution)/shard_map/ppermute | solution.py:210
  217.4 4.9 %collective-permute-start.8 = (f32[2,2,1,8]{3,2,1,0:T(1,128)S(1)}, f32[2,2,1,8]{3,2,1,0:T(1,128)S(1)}, u32[]{:S(2)}, u32[]{:S(2)}) collective-permute-start(f32[2,2,1,8]{3,2,1,0:T(1,128)S(1)} %get-tuple-element.115), channel_id=1, source_target_pairs={{4,0},{8,4},{12,8},{16,12},{20,16},{24,20},{28,24},{32,28},{36,32}... | collective-permute-start | bytes 392 | tf_op jit(solution)/shard_map/ppermute | solution.py:212
  222.5 29.9 %copy-start.4 = (f32[2,2,8,8]{3,2,1,0:T(8,128)}, f32[2,2,8,8]{3,2,1,0:T(8,128)S(1)}, u32[]{:S(2)}) copy-start(f32[2,2,8,8]{3,2,1,0:T(8,128)S(1)} %get-tuple-element.109) | copy-start | bytes 3076

commit v2 on v1

v2 whole, which is shorter than its diff:
```python
import functools
import math

import jax
import jax.numpy as jnp
from jax import lax
from jax.experimental import pallas as pl
from jax.experimental.pallas import tpu as pltpu
from jax.sharding import PartitionSpec as P

C = 64
TILE = 32
MAXD = 7
R = 1
SMOOTH = 3
HALO = 64
BF = jnp.bfloat16
F32 = jnp.float32


def lane_pick(scalars, lanes_tile):
    out = jnp.full(lanes_tile.shape, scalars[0])
    for t in range(1, len(scalars)):
        out = jnp.where(lanes_tile == t, scalars[t], out)
    return out


NEAR = 16
WINDOW = 3


def score_rows(f_rows, window, coarse_row, coarse_col, left, right, count):
    src = lax.broadcasted_iota(jnp.int32, (256, 128), 0)
    lane = lax.broadcasted_iota(jnp.int32, (1, 128), 1)
    lane_tile = lane // TILE
    shifts = []
    for h in range(2):
        col = lane + 128 * h + lane_pick([coarse_col[4 * h + t] for t in range(4)], lane_tile)
        rel = src - col
        for b in (-1, 0, 1):
            shifts.append(jnp.where(rel == b, 1.0, 0.0).astype(BF))
    shifted = jnp.concatenate(shifts, 1)
    for c0 in range(0, count, 4):
        moved = lax.dot_general(
            window(c0), shifted, (((1,), (0,)), ((), ())), preferred_element_type=F32
        ).astype(BF)
        for c in range(4):
            for h in range(2):
                for b in range(3):
                    right[h, 64 * b : 64 * b + 64, 128 * (c0 + c) : 128 * (c0 + c) + 128] = moved[
                        64 * c : 64 * c + 64, 384 * h + 128 * b : 384 * h + 128 * b + 128
                    ]
    tile_masks = [lax.broadcasted_iota(jnp.int32, (TILE, 128), 1) // TILE == t for t in range(4)]
    for c in range(count):
        strip = f_rows(c)
        for h in range(2):
            part = strip[:, 128 * h : 128 * h + 128]
            for t in range(4):
                left[h, TILE * t : TILE * t + TILE, 128 * c : 128 * c + 128] = jnp.where(
                    tile_masks[t], part, jnp.zeros_like(part)
                )
    row = lax.broadcasted_iota(jnp.int32, (128, 192), 0)
    col = lax.broadcasted_iota(jnp.int32, (128, 192), 1)
    base = col % 64 - NEAR - row % TILE
    row_tile = lax.broadcasted_iota(jnp.int32, (128, 1), 0) // TILE
    out = [[], [], []]
    for h in range(2):
        gram = lax.dot_general(
            left[h, :, : count * 128],
            right[h, :, : count * 128],
            (((1,), (1,)), ((), ())),
            preferred_element_type=F32,
        )
        rel = base - lane_pick([coarse_row[4 * h + t] for t in range(4)], row_tile)
        for a in range(3):
            kept = jnp.where(rel == a - 1, gram, 0.0)
            out[a].append(jnp.sum(kept.reshape(4, TILE, 192), axis=1))
    return [jnp.concatenate(o, 0) for o in out]


def gather_offsets(acc):
    total = jnp.zeros((16, 128), F32)
    seg = lax.broadcasted_iota(jnp.int32, (16, 192), 1) // 64
    row = lax.broadcasted_iota(jnp.int32, (16, 192), 0)
    for a in range(3):
        pick = (row == seg + 3 * a).astype(F32)
        total = total + lax.dot_general(
            pick, acc[a], (((1,), (1,)), ((), ())), precision=lax.Precision.HIGHEST, preferred_element_type=F32
        )
    return total


def drift_kernel(
    devices, cs, cv, feat,
    field_out, whole_out, frac_out, top_out, bottom_out,
    own, prior, later, later_coarse, later_cs, left, right, acc, acc_later,
    q_send, b_send, q_slots, b_slots, e_send, e_slots,
    load_sem, near_s, near_r, far_s, far_r, edge_s, edge_r, cc_s, cc_r, cc_l,
    a_s, a_r, b_s, b_r, d_s, d_r, g_s, g_r, e_s, e_r, keep_sem,
):
    secs, areas, chans = devices
    k, i, j = (lax.axis_index(name) for name in ("sec", "area", "chan"))
    MESH = pl.DeviceIdType.MESH

    def at(sec, area, chan):
        return {"sec": sec, "area": area, "chan": chan}

    def remote(src, dst, send, recv, target):
        return pltpu.make_async_remote_copy(
            src_ref=src, dst_ref=dst, send_sem=send, recv_sem=recv, device_id=target, device_id_type=MESH
        )

    nxt, prv = lax.rem(k + 1, secs), lax.rem(k + secs - 1, secs)
    down, up = lax.rem(i + 1, areas), lax.rem(i + areas - 1, areas)
    has_next, has_prev = k < secs - 1, k > 0
    has_down, has_up = i < areas - 1, i > 0

    loads = [
        pltpu.make_async_copy(feat.at[s], own.at[s, :, pl.ds(NEAR, 256), :], load_sem.at[s]) for s in range(2)
    ]
    for load in loads:
        load.start()

    barrier = pltpu.get_barrier_semaphore()
    for other in range(secs):
        for side, there in ((-1, has_up), (0, True), (1, has_down)):
            fits = jnp.logical_and(there, jnp.logical_or(side != 0, k != other))

            @pl.when(fits)
            def _():
                pl.semaphore_signal(barrier, inc=1, device_id=at(other, i + side, j), device_id_type=MESH)

    for step, there in ((-1, has_prev), (0, True), (1, has_next)):
        for turn in range(1, chans):

            @pl.when(there)
            def _():
                pl.semaphore_signal(
                    barrier, inc=1, device_id=at(k + step, i, lax.rem(j + turn, chans)), device_id_type=MESH
                )

    one = lambda flag: jnp.where(flag, 1, 0)
    pl.semaphore_wait(
        barrier,
        secs * (1 + one(has_up) + one(has_down)) - 1 + (chans - 1) * (1 + one(has_prev) + one(has_next)),
    )

    near_down = remote(
        feat.at[:, :, pl.ds(256 - NEAR, NEAR), :], own.at[:, :, pl.ds(0, NEAR), :], near_s.at[0], near_r.at[0], at(k, down, j)
    )
    near_up = remote(
        feat.at[:, :, pl.ds(0, NEAR), :], own.at[:, :, pl.ds(NEAR + 256, NEAR), :], near_s.at[1], near_r.at[1], at(k, up, j)
    )
    edge_down = remote(
        feat.at[1, pl.ds(0, 8), pl.ds(256 - NEAR, NEAR), :], prior.at[:, pl.ds(0, NEAR), :], edge_s.at[0], edge_r.at[0], at(nxt, down, j)
    )
    edge_up = remote(
        feat.at[1, pl.ds(0, 8), pl.ds(0, NEAR), :], prior.at[:, pl.ds(NEAR + 256, NEAR), :], edge_s.at[1], edge_r.at[1], at(nxt, up, j)
    )
    coarse_back = remote(cv, later_coarse, cc_s, cc_r, at(prv, i, j))

    def far_down(r):
        rows = HALO - 16 * (r + 1)
        return remote(
            feat.at[:, :, pl.ds(240 - 16 * r, 16), :], top_out.at[:, :, pl.ds(rows, 16), :], far_s.at[0, r], far_r.at[0, r], at(k, down, j)
        )

    def far_up(r):
        return remote(
            feat.at[:, :, pl.ds(16 * r, 16), :], bottom_out.at[:, :, pl.ds(16 * r, 16), :], far_s.at[1, r], far_r.at[1, r], at(k, up, j)
        )

    def ahead(c):
        return remote(
            feat.at[1, pl.ds(0, 8), pl.ds(pl.multiple_of(TILE * c, TILE), TILE), :],
            prior.at[:, pl.ds(pl.multiple_of(NEAR + TILE * c, NEAR), TILE), :],
            a_s.at[c], a_r.at[c], at(nxt, i, j),
        )

    def behind(c):
        return remote(
            feat.at[0, pl.ds(8, 8), pl.ds(pl.multiple_of(TILE * c, TILE), TILE), :],
            later.at[:, pl.ds(pl.multiple_of(TILE * c, TILE), TILE), :],
            b_s.at[c], b_r.at[c], at(prv, i, j),
        )

    def start_parts(c):
        @pl.when(has_next)
        def _():
            ahead(c).start()

        @pl.when(has_prev)
        def _():
            behind(c).start()

    def start_far():
        for r in range(1, 4):

            @pl.when(jnp.logical_and(has_down, k >= r))
            def _():
                far_down(r).start()

            @pl.when(jnp.logical_and(has_up, k >= r))
            def _():
                far_up(r).start()

    @pl.when(has_down)
    def _():
        near_down.start()

    @pl.when(has_up)
    def _():
        near_up.start()

    @pl.when(has_prev)
    def _():
        coarse_back.start()

    @pl.when(jnp.logical_and(has_next, has_down))
    def _():
        edge_down.start()

    @pl.when(jnp.logical_and(has_next, has_up))
    def _():
        edge_up.start()

    for c in range(WINDOW):
        start_parts(c)

    @pl.when(jnp.logical_not(has_next))
    def _():
        start_far()

    @pl.when(jnp.logical_not(has_up))
    def _():
        own[:, :, pl.ds(0, NEAR), :] = jnp.zeros((2, 16, NEAR, 256), BF)
        prior[:, pl.ds(0, NEAR), :] = jnp.zeros((8, NEAR, 256), BF)

    @pl.when(jnp.logical_not(has_down))
    def _():
        own[:, :, pl.ds(NEAR + 256, NEAR), :] = jnp.zeros((2, 16, NEAR, 256), BF)
        prior[:, pl.ds(NEAR + 256, NEAR), :] = jnp.zeros((8, NEAR, 256), BF)

    acc[...] = jnp.zeros_like(acc)
    acc_later[...] = jnp.zeros_like(acc_later)
    for load in loads:
        load.wait()

    keep_top = pltpu.make_async_copy(
        own.at[:, :, pl.ds(0, NEAR), :], top_out.at[:, :, pl.ds(HALO - NEAR, NEAR), :], keep_sem.at[0]
    )
    keep_bottom = pltpu.make_async_copy(
        own.at[:, :, pl.ds(NEAR + 256, NEAR), :], bottom_out.at[:, :, pl.ds(0, NEAR), :], keep_sem.at[1]
    )

    @pl.when(has_up)
    def _():
        near_down.wait_recv()

    @pl.when(has_down)
    def _():
        near_up.wait_recv()

    keep_top.start()
    keep_bottom.start()

    def local_row(ty, _):
        top = pl.multiple_of(ty * TILE, TILE)
        blocks = score_rows(
            lambda c: own[1, c, pl.ds(pl.multiple_of(top + NEAR, NEAR), TILE), :],
            lambda c: own[0, c : c + 4, pl.ds(top, 64), :].reshape(256, 256),
            [cs[0, 64 + ty * 8 + t] for t in range(8)],
            [cs[1, 64 + ty * 8 + t] for t in range(8)],
            left, right, 16,
        )
        for a in range(3):
            acc[a, pl.ds(pl.multiple_of(64 + ty * 8, 8), 8), :] = blocks[a]
        return 0

    lax.fori_loop(0, 8, local_row, 0)

    coarse_local = pltpu.make_async_copy(later_coarse, later_cs, cc_l)

    @pl.when(has_next)
    def _():
        coarse_back.wait_recv()
        coarse_local.start()
        coarse_local.wait()

    @pl.when(has_prev)
    def _():
        ahead(0).wait_recv()

        @pl.when(has_up)
        def _():
            edge_down.wait_recv()

        @pl.when(has_down)
        def _():
            edge_up.wait_recv()

    def remote_row(ty, _):
        top = pl.multiple_of(ty * TILE, TILE)

        @pl.when(has_prev)
        def _():
            @pl.when(ty < 7)
            def _():
                ahead(ty + 1).wait_recv()

            behind(ty).wait_send()

        @pl.when(has_next)
        def _():
            behind(ty).wait_recv()
            ahead(ty).wait_send()

        @pl.when(ty + WINDOW < 8)
        def _():
            start_parts(ty + WINDOW)

        @pl.when(has_prev)
        def _():
            blocks = score_rows(
                lambda c: own[0, c, pl.ds(pl.multiple_of(top + NEAR, NEAR), TILE), :],
                lambda c: prior[c : c + 4, pl.ds(top, 64), :].reshape(256, 256),
                [cs[0, ty * 8 + t] for t in range(8)],
                [cs[1, ty * 8 + t] for t in range(8)],
                left, right, 8,
            )
            for a in range(3):
                acc[a, pl.ds(pl.multiple_of(ty * 8, 8), 8), :] = blocks[a]

        @pl.when(has_next)
        def _():
            blocks = score_rows(
                lambda c: later[c, pl.ds(top, TILE), :],
                lambda c: own[1, 8 + c : 12 + c, pl.ds(top, 64), :].reshape(256, 256),
                [later_cs[0, ty * 8 + t] for t in range(8)],
                [later_cs[1, ty * 8 + t] for t in range(8)],
                left, right, 8,
            )
            for a in range(3):
                acc_later[a, pl.ds(pl.multiple_of(ty * 8, 8), 8), :] = blocks[a]

        return 0

    lax.fori_loop(0, 8, remote_row, 0)

    mine = gather_offsets(acc)
    q_send[...] = mine
    q_slots[j] = mine
    b_send[...] = gather_offsets(acc_later)

    def share(turn):
        return remote(q_send, q_slots.at[j], d_s.at[turn], d_r.at[turn], at(k, i, lax.rem(j + turn, chans)))

    def give(turn):
        return remote(b_send, b_slots.at[j], g_s.at[turn], g_r.at[turn], at(nxt, i, lax.rem(j + turn, chans)))

    for turn in range(chans):

        @pl.when(has_next)
        def _():
            give(turn).start()

        if turn:
            share(turn).start()

    @pl.when(has_next)
    def _():
        start_far()

    for turn in range(chans):
        if turn:
            share(turn).wait_recv()

        @pl.when(has_prev)
        def _():
            give(turn).wait_recv()

    total = jnp.zeros((16, 128), F32)
    for chan in range(chans):
        total = total + q_slots[chan]
    for chan in range(chans):
        total = total + jnp.where(has_prev, b_slots[chan], 0.0)
    scores = total * (1.0 / math.sqrt(C * TILE * TILE))
    row = lax.broadcasted_iota(jnp.int32, (16, 128), 0)
    weights = jnp.where(row < 9, 1.0 / (1.0 + jnp.exp(-scores)), 0.0)
    weight_total = jnp.sum(weights, axis=0, keepdims=True)
    fine_row = jnp.sum(weights * (row // 3 - 1).astype(F32), axis=0, keepdims=True) / weight_total
    fine_col = jnp.sum(weights * (row % 3 - 1).astype(F32), axis=0, keepdims=True) / weight_total
    lane = lax.broadcasted_iota(jnp.int32, (8, 128), 1)
    comp = lax.broadcasted_iota(jnp.int32, (8, 128), 0)
    moved = cv[...].astype(F32)
    pair = jnp.where(comp == 0, moved[0:1] + fine_row, moved[1:2] + fine_col)
    pair = jnp.where(jnp.logical_and(comp < 2, jnp.logical_or(has_prev, lane >= 64)), pair, 0.0)
    e_send[...] = pair
    e_slots[k * 3 + 1] = pair

    def tell(ahead_by, side):
        slot = k * 3 + 1 - side
        return remote(
            e_send, e_slots.at[slot], e_s.at[ahead_by, side + 1], e_r.at[slot],
            at(lax.rem(k + ahead_by, secs), lax.rem(i + side + areas, areas), j),
        )

    sides = ((-1, has_up), (0, True), (1, has_down))
    messages = [
        (ahead_by, side, jnp.logical_and(there, k + ahead_by < secs))
        for ahead_by in range(secs)
        for side, there in sides
        if ahead_by or side
    ]
    for ahead_by, side, fits in messages:

        @pl.when(fits)
        def _():
            tell(ahead_by, side).start()

    def hear(sec, side):
        return remote(
            e_send, e_slots.at[sec * 3 + 1 + side], e_s.at[0, 0], e_r.at[sec * 3 + 1 + side], at(prv, i, j)
        )

    for sec in range(secs):
        for side, there in sides:
            fits = jnp.logical_and(there, sec <= k if side else sec < k)

            @pl.when(fits)
            def _():
                hear(sec, side).wait_recv()

    roll = lambda x, by: pltpu.roll(x, by, 1)
    fields = []
    for side, there in sides:
        earlier = jnp.zeros((8, 128), F32)
        for sec in range(secs - 1):
            earlier = earlier + jnp.where(sec < k, e_slots[sec * 3 + 1 + side], 0.0)
        here = e_slots[k * 3 + 1 + side]
        summed = here + jnp.where(lane >= 64, roll(here, 64), 0.0) + (earlier + roll(earlier, 64))
        fields.append(jnp.where(there, summed, 0.0) if side else summed)
    tile_row, tile_col = lane % 64 // 8, lane % 8
    outside = (has_up, True, has_down)
    for sweep in range(SMOOTH):
        new = []
        for n in range(3):
            x = fields[n]
            above = roll(x, 8)
            below = roll(x, 120)
            if n > 0:
                above = jnp.where(tile_row == 0, roll(fields[n - 1], 72), above)
            if n < 2:
                below = jnp.where(tile_row == 7, roll(fields[n + 1], 56), below)
            west = jnp.where(tile_col > 0, roll(x, 1), 0.0)
            east = jnp.where(tile_col < 7, roll(x, 127), 0.0)
            grid_row = (i + n - 1) * 8 + tile_row
            count = (
                (grid_row > 0).astype(F32)
                + (grid_row < areas * 8 - 1).astype(F32)
                + (tile_col > 0).astype(F32)
                + (tile_col < 7).astype(F32)
            )
            above = jnp.where(grid_row > 0, above, 0.0)
            below = jnp.where(grid_row < areas * 8 - 1, below, 0.0)
            mean = (x + (above + below + west + east)) / (1.0 + count)
            new.append(mean if n == 1 else jnp.where(outside[n], mean, 0.0))
        fields = new
    field = fields[1]
    floors = jnp.floor(field)
    field_out[...] = field[0:2]
    whole_out[...] = floors[0:2].astype(jnp.int32)
    frac_out[...] = (field - floors)[0:2]

    for turn in range(chans):
        if turn:
            share(turn).wait_send()

        @pl.when(has_next)
        def _():
            give(turn).wait_send()

    for ahead_by, side, fits in messages:

        @pl.when(fits)
        def _():
            tell(ahead_by, side).wait_send()

    @pl.when(has_down)
    def _():
        near_down.wait_send()

    @pl.when(has_up)
    def _():
        near_up.wait_send()

    @pl.when(has_prev)
    def _():
        coarse_back.wait_send()

    @pl.when(jnp.logical_and(has_next, has_down))
    def _():
        edge_down.wait_send()

    @pl.when(jnp.logical_and(has_next, has_up))
    def _():
        edge_up.wait_send()

    for r in range(1, 4):

        @pl.when(jnp.logical_and(has_down, k >= r))
        def _():
            far_down(r).wait_send()
            far_up(r).wait_recv()

        @pl.when(jnp.logical_and(has_up, k >= r))
        def _():
            far_up(r).wait_send()
            far_down(r).wait_recv()

    keep_top.wait()
    keep_bottom.wait()


def drift_local(devices, coarse, features):
    vm = pl.BlockSpec(memory_space=pltpu.VMEM)
    sm = pl.BlockSpec(memory_space=pltpu.SMEM)
    hbm = pl.BlockSpec(memory_space=pl.ANY)
    dma = pltpu.SemaphoreType.DMA
    small = jax.ShapeDtypeStruct((2, 128), F32)
    halo = jax.ShapeDtypeStruct((2, 16, HALO, 256), BF)
    secs, areas, chans = devices
    return pl.pallas_call(
        functools.partial(drift_kernel, devices),
        out_shape=(small, jax.ShapeDtypeStruct((2, 128), jnp.int32), small, halo, halo),
        in_specs=[sm, vm, hbm],
        out_specs=(vm, vm, vm, hbm, hbm),
        scratch_shapes=[
            pltpu.VMEM((2, 16, 256 + 2 * NEAR, 256), BF),
            pltpu.VMEM((8, 256 + 2 * NEAR, 256), BF),
            pltpu.VMEM((8, 256, 256), BF),
            pltpu.VMEM((2, 128), jnp.int32),
            pltpu.SMEM((2, 128), jnp.int32),
            pltpu.VMEM((2, 128, 2048), BF),
            pltpu.VMEM((2, 192, 2048), BF),
            pltpu.VMEM((3, 128, 192), F32),
            pltpu.VMEM((3, 128, 192), F32),
            pltpu.VMEM((16, 128), F32),
            pltpu.VMEM((16, 128), F32),
            pltpu.VMEM((chans, 16, 128), F32),
            pltpu.VMEM((chans, 16, 128), F32),
            pltpu.VMEM((8, 128), F32),
            pltpu.VMEM((3 * secs, 8, 128), F32),
            dma((2,)), dma((2,)), dma((2,)), dma((2, 4)), dma((2, 4)), dma((2,)), dma((2,)), dma, dma, dma,
            dma((8,)), dma((8,)), dma((8,)), dma((8,)),
            dma((chans,)), dma((chans,)), dma((chans,)), dma((chans,)),
            dma((secs, 3)), dma((3 * secs,)), dma((2,)),
        ],
        compiler_params=pltpu.CompilerParams(
            collective_id=0, has_side_effects=True, vmem_limit_bytes=48 * 2**20
        ),
        name="drift",
    )(coarse, coarse, features)


def warp_kernel(areas, whole, frac, field, feat, top_halo, bottom_halo, out_ref, field_out, held, rows, sems):
    step = pl.program_id(0)
    s = step // 8
    ty = step % 8
    i = lax.axis_index("area")

    def load(part):
        return [
            pltpu.make_async_copy(feat.at[part], held.at[part, :, pl.ds(HALO, 256), :], sems.at[part, 0]),
            pltpu.make_async_copy(top_halo.at[part], held.at[part, :, pl.ds(0, HALO), :], sems.at[part, 1]),
            pltpu.make_async_copy(bottom_halo.at[part], held.at[part, :, pl.ds(HALO + 256, HALO), :], sems.at[part, 2]),
        ]

    def wait(part):
        for copy in load(part):
            copy.wait()

        @pl.when(i == 0)
        def _():
            held[part, :, pl.ds(0, HALO), :] = jnp.zeros((16, HALO, 256), BF)

        @pl.when(i == areas - 1)
        def _():
            held[part, :, pl.ds(HALO + 256, HALO), :] = jnp.zeros((16, HALO, 256), BF)

    @pl.when(step == 0)
    def _():
        for part in range(2):
            for copy in load(part):
                copy.start()
        lane = lax.broadcasted_iota(jnp.int32, (32, 128), 1)
        row = lax.broadcasted_iota(jnp.int32, (32, 128), 0)
        spread = jnp.where(row < 16, field[0:1, :], field[1:2, :])
        spread = jnp.where(lane // 8 == row % 16, spread, 0.0)
        pick = lax.broadcasted_iota(jnp.int32, (128, 8), 0) % 8 == lax.broadcasted_iota(jnp.int32, (128, 8), 1)
        grid = jnp.dot(
            spread, pick.astype(F32), precision=lax.Precision.HIGHEST, preferred_element_type=F32
        )
        field_out[...] = grid.reshape(2, 2, 8, 8)
        wait(0)

    @pl.when(step == 8)
    def _():
        wait(1)

    lane = lax.broadcasted_iota(jnp.int32, (1, 128), 1)
    lane_tile = lane // TILE
    src_col = lax.broadcasted_iota(jnp.int32, (256, 128), 0)
    base = HALO + TILE * ty
    for h in range(2):
        at = step * 8 + 4 * h
        fl_row = [whole[0, at + t] for t in range(4)]
        fl_col = [whole[1, at + t] for t in range(4)]
        fr_row = lane_pick([frac[0, at + t] for t in range(4)], lane_tile)
        fr_col = lane_pick([frac[1, at + t] for t in range(4)], lane_tile)
        low = jnp.minimum(jnp.minimum(fl_row[0], fl_row[1]), jnp.minimum(fl_row[2], fl_row[3]))
        high = jnp.maximum(jnp.maximum(fl_row[0], fl_row[1]), jnp.maximum(fl_row[2], fl_row[3]))
        start = jnp.minimum((base + low) // 16 * 16, 2 * HALO + 256 - 48)
        chunks = (base + high + TILE + 1 - start + 15) // 16
        rel = src_col - (lane + 128 * h + lane_pick(fl_col, lane_tile))
        weight = jnp.where(rel == 0, 1.0 - fr_col, jnp.where(rel == 1, fr_col, 0.0))
        coarse_part = weight.astype(BF)
        fine_part = (weight - coarse_part.astype(F32)).astype(BF)
        mixer = jnp.concatenate([coarse_part, fine_part], 1)

        def chunk(r, _):
            at_row = pl.multiple_of(start + 16 * r, 16)
            block = held[s, :, pl.ds(at_row, 16), :].reshape(256, 256)
            mixed = jnp.dot(block, mixer, preferred_element_type=F32)
            mixed = mixed[:, :128] + mixed[:, 128:]
            rows[:, pl.ds(pl.multiple_of(16 * r, 16), 16), :] = mixed.reshape(16, 16, 128)
            return 0

        for r in range(3):
            chunk(r, 0)
        lax.fori_loop(3, chunks, chunk, 0)
        offs = [base + fl_row[t] - start for t in range(4)]
        for c in range(16):
            upper = rows[c, pl.ds(offs[0], TILE), :]
            lower = rows[c, pl.ds(offs[0] + 1, TILE), :]
            for t in range(1, 4):
                mine = lane_tile == t
                upper = jnp.where(mine, rows[c, pl.ds(offs[t], TILE), :], upper)
                lower = jnp.where(mine, rows[c, pl.ds(offs[t] + 1, TILE), :], lower)
            out_ref[0, c, :, 128 * h : 128 * h + 128] = ((1.0 - fr_row) * upper + fr_row * lower).astype(BF)


def warp_local(areas, whole, frac, field, features, top_halo, bottom_halo):
    sm = pl.BlockSpec(memory_space=pltpu.SMEM)
    hbm = pl.BlockSpec(memory_space=pl.ANY)
    return pl.pallas_call(
        functools.partial(warp_kernel, areas),
        grid=(16,),
        out_shape=(
            jax.ShapeDtypeStruct((2, 16, 256, 256), BF),
            jax.ShapeDtypeStruct((2, 2, 8, 8), F32),
        ),
        in_specs=[sm, sm, pl.BlockSpec(memory_space=pltpu.VMEM), hbm, hbm, hbm],
        out_specs=(
            pl.BlockSpec((1, 16, TILE, 256), lambda g: (g // 8, 0, g % 8, 0)),
            pl.BlockSpec(memory_space=pltpu.VMEM),
        ),
        scratch_shapes=[
            pltpu.VMEM((2, 16, 2 * HALO + 256, 256), BF),
            pltpu.VMEM((16, 176, 128), F32),
            pltpu.SemaphoreType.DMA((2, 3)),
        ],
        compiler_params=pltpu.CompilerParams(vmem_limit_bytes=48 * 2**20),
        name="warp",
    )(whole, frac, field, features, top_halo, bottom_halo)


def local(devices, features, coarse):
    field, whole, frac, top_halo, bottom_halo = drift_local(devices, coarse.reshape(2, 128), features)
    return warp_local(devices[1], whole, frac, field, features, top_halo, bottom_halo)


def solution(mesh):
    placed = (P("sec", "chan", "area", None), P(None, "sec", "area", None))
    devices = tuple(mesh.shape[name] for name in ("sec", "area", "chan"))
    return jax.shard_map(
        functools.partial(local, devices),
        mesh=mesh,
        in_specs=placed,
        out_specs=placed,
        check_vma=False,
    )
```

time: 253 us -> 114 us (0.45)
  waiting for transfers between devices: 84.3 us -> 0 us
  blocking collectives: 73.3 us -> 0 us
  Pallas kernels: 53 us -> 112 us
  starting transfers between devices: 28.1 us -> 0 us
  local copies, waits for them, and re-layouts: 12.1 us -> 0.8 us
    ppermute x9 -> x0, waiting for transfers between devices: 84.3 us -> none  [the longest x1 54.1 us: shifted(): return lax.ppermute(shard, axis, pairs)]
    pallas_call x2, Pallas kernels: 53 us -> 112 us  [the longest x1 85.1 us: drift_local(): pl.pallas_call(functools.partial(drift_kernel, devices), out_shape=(small...]
    all_gather x1 -> x0, blocking collectives: 59 us -> none  [prefix(): pieces = lax.all_gather(value, axis)]
    ppermute x9 -> x0, starting transfers between devices: 28.1 us -> none  [the longest x4 18.2 us: padded_2(): lax.ppermute(tail, axis, [(i, (i + 1) % count) for i in range(ends)])]
    psum x1 -> x0, blocking collectives: 14.3 us -> none  [local(): scores = lax.psum(partial_scores, 'chan') * score_scale]
    unnamed x12 -> x0, local copies, waits for them, and re-layouts: 4.67 us -> none
    squeeze x1 -> x0, local copies, waits for them, and re-layouts: 2.65 us -> none  [local(): own[0, :, HALO - 16:HALO + 272]]
    slice x6 -> x0, local copies, waits for them, and re-layouts: 2.57 us -> none  [the longest x1 1.84 us: padded_2(): head = lax.slice_in_dim(cells, 0, width, axis=dim)]
  transfers between devices with their start and end apart: 9 -> 0, of which waited for: 6 -> 0; matrix products, arithmetic and copies ran while one was open for 1% -> 0% of each run, Pallas kernels for 0% -> 0%
where the time goes in v2:
time: 114 us
  Pallas kernels  112 us (98%)
    pallas_call x1, Pallas kernels, drift_local(): pl.pallas_call(functools.partial(drift_kernel, devices), out_shape=(small...  85.1 us
    pallas_call x1, Pallas kernels, warp_local(): pl.pallas_call(functools.partial(warp_kernel, areas), grid=(16,), out_sha...  27 us

profile of v2, /device:TPU:197, one launch (start us, length us, event | category | flops | bytes accessed | tf_op | source)
XLA Modules:
  0.0 113.5 jit_solution(15221539968728001294)
XLA Ops:
  0.6 0.8 reshape.7.cs.cv
  1.4 85.1 %drift.1 = (f32[2,128]{1,0:T(2,128)S(1)}, s32[2,128]{1,0:T(2,128)S(1)}, f32[2,128]{1,0:T(2,128)S(1)}, bf16[2,16,64,256]{3,2,1,0:T(8,128)(2,1)S(1)}, bf16[2,16,64,256]{3,2,1,0:T(8,128)(2,1)S(1)}) custom-call(s32[2,128]{1,0:T(2,128)S(1)} %reshape.7.cs.cv, s32[2,128]{1,0:T(2,128)S(1)} %reshape.7.cs.cv, bf16[2,16,256,256]{3,2,1,0:T(8,128)(2,1)} %feat.3), custom_call_target="tpu_custom_call" | custom-call | tf_op jit(solution)/shard_map/drift/pallas_call | solution.py:533
  86.5 27.0 %warp.1 = (bf16[2,16,256,256]{3,2,1,0:T(8,128)(2,1)}, f32[2,2,8,8]{3,2,1,0:T(8,128)}) custom-call(s32[2,128]{1,0:T(2,128)S(1)} %get-tuple-element.7.whole, f32[2,128]{1,0:T(2,128)S(1)} %get-tuple-element.8.frac, f32[2,128]{1,0:T(2,128)S(1)} %get-tuple-element.9.field, bf16[2,16,256,256]{3,2,1,0:T(8,128)(2,1)} %feat.3, ...), custom_call_target="tpu_custom_call" | custom-call | tf_op jit(solution)/shard_map/warp/pallas_call | solution.py:656

commit v3 on v2

--- a/solution.py
+++ b/solution.py
@@ -26,7 +26,7 @@
 
 
 NEAR = 16
-WINDOW = 3
+WINDOW = 8
 
 
 def score_rows(f_rows, window, coarse_row, coarse_col, left, right, count):
@@ -145,29 +145,44 @@
         secs * (1 + one(has_up) + one(has_down)) - 1 + (chans - 1) * (1 + one(has_prev) + one(has_next)),
     )
 
-    near_down = remote(
-        feat.at[:, :, pl.ds(256 - NEAR, NEAR), :], own.at[:, :, pl.ds(0, NEAR), :], near_s.at[0], near_r.at[0], at(k, down, j)
+    heads, tails = pl.ds(0, NEAR), pl.ds(256 - NEAR, NEAR)
+    above, below = pl.ds(0, NEAR), pl.ds(NEAR + 256, NEAR)
+    near_chans = (pl.ds(0, 16), pl.ds(8, 8))
+
+    def near_down(s):
+        return remote(
+            feat.at[s, near_chans[s], tails, :], own.at[s, near_chans[s], above, :], near_s.at[0, s], near_r.at[0, s], at(k, down, j)
+        )
+
+    def near_up(s):
+        return remote(
+            feat.at[s, near_chans[s], heads, :], own.at[s, near_chans[s], below, :], near_s.at[1, s], near_r.at[1, s], at(k, up, j)
+        )
+
+    relay_up = remote(
+        prior.at[:, pl.ds(NEAR, NEAR), :], prior.at[:, below, :], edge_s.at[1], edge_r.at[1], at(k, up, j)
     )
-    near_up = remote(
-        feat.at[:, :, pl.ds(0, NEAR), :], own.at[:, :, pl.ds(NEAR + 256, NEAR), :], near_s.at[1], near_r.at[1], at(k, up, j)
-    )
-    edge_down = remote(
-        feat.at[1, pl.ds(0, 8), pl.ds(256 - NEAR, NEAR), :], prior.at[:, pl.ds(0, NEAR), :], edge_s.at[0], edge_r.at[0], at(nxt, down, j)
-    )
-    edge_up = remote(
-        feat.at[1, pl.ds(0, 8), pl.ds(0, NEAR), :], prior.at[:, pl.ds(NEAR + 256, NEAR), :], edge_s.at[1], edge_r.at[1], at(nxt, up, j)
+    relay_down = remote(
+        prior.at[:, pl.ds(256, NEAR), :], prior.at[:, above, :], edge_s.at[0], edge_r.at[0], at(k, down, j)
     )
     coarse_back = remote(cv, later_coarse, cc_s, cc_r, at(prv, i, j))
 
-    def far_down(r):
-        rows = HALO - 16 * (r + 1)
+    far_parts = [(1, 0, 8, 0), (0, 1, 16, 2), (1, 1, 16, 1), (0, 2, 16, 3), (1, 2, 16, 2), (1, 3, 16, 3)]
+
+    def far_down(n):
+        s, r, channels, _ = far_parts[n]
         return remote(
-            feat.at[:, :, pl.ds(240 - 16 * r, 16), :], top_out.at[:, :, pl.ds(rows, 16), :], far_s.at[0, r], far_r.at[0, r], at(k, down, j)
-        )
-
-    def far_up(r):
+            feat.at[s, pl.ds(0, channels), pl.ds(240 - 16 * r, 16), :],
+            top_out.at[s, pl.ds(0, channels), pl.ds(HALO - 16 * (r + 1), 16), :],
+            far_s.at[0, n], far_r.at[0, n], at(k, down, j),
+        )
+
+    def far_up(n):
+        s, r, channels, _ = far_parts[n]
         return remote(
-            feat.at[:, :, pl.ds(16 * r, 16), :], bottom_out.at[:, :, pl.ds(16 * r, 16), :], far_s.at[1, r], far_r.at[1, r], at(k, up, j)
+            feat.at[s, pl.ds(0, channels), pl.ds(16 * r, 16), :],
+            bottom_out.at[s, pl.ds(0, channels), pl.ds(16 * r, 16), :],
+            far_s.at[1, n], far_r.at[1, n], at(k, up, j),
         )
 
     def ahead(c):
@@ -194,38 +209,35 @@
             behind(c).start()
 
     def start_far():
-        for r in range(1, 4):
-
-            @pl.when(jnp.logical_and(has_down, k >= r))
+        for n, (_, _, _, first) in enumerate(far_parts):
+
+            @pl.when(jnp.logical_and(has_down, k >= first))
             def _():
-                far_down(r).start()
-
-            @pl.when(jnp.logical_and(has_up, k >= r))
+                far_down(n).start()
+
+            @pl.when(jnp.logical_and(has_up, k >= first))
             def _():
-                far_up(r).start()
-
-    @pl.when(has_down)
-    def _():
-        near_down.start()
-
-    @pl.when(has_up)
-    def _():
-        near_up.start()
+                far_up(n).start()
+
+    def part_of(n):
+        return jnp.where(n == 0, 0, jnp.where(n == 1, 7, n - 1))
+
+    for s in range(2):
+
+        @pl.when(has_down)
+        def _():
+            near_down(s).start()
+
+        @pl.when(has_up)
+        def _():
+            near_up(s).start()
 
     @pl.when(has_prev)
     def _():
         coarse_back.start()
 
-    @pl.when(jnp.logical_and(has_next, has_down))
-    def _():
-        edge_down.start()
-
-    @pl.when(jnp.logical_and(has_next, has_up))
-    def _():
-        edge_up.start()
-
-    for c in range(WINDOW):
-        start_parts(c)
+    for n in range(WINDOW):
+        start_parts(part_of(n))
 
     @pl.when(jnp.logical_not(has_next))
     def _():
@@ -246,23 +258,25 @@
     for load in loads:
         load.wait()
 
-    keep_top = pltpu.make_async_copy(
-        own.at[:, :, pl.ds(0, NEAR), :], top_out.at[:, :, pl.ds(HALO - NEAR, NEAR), :], keep_sem.at[0]
-    )
-    keep_bottom = pltpu.make_async_copy(
-        own.at[:, :, pl.ds(NEAR + 256, NEAR), :], bottom_out.at[:, :, pl.ds(0, NEAR), :], keep_sem.at[1]
-    )
-
-    @pl.when(has_up)
-    def _():
-        near_down.wait_recv()
-
-    @pl.when(has_down)
-    def _():
-        near_up.wait_recv()
-
-    keep_top.start()
-    keep_bottom.start()
+    keeps = [
+        pltpu.make_async_copy(
+            own.at[s, near_chans[s], rows, :], halo.at[s, near_chans[s], pl.ds(first, NEAR), :], keep_sem.at[s, side]
+        )
+        for s in range(2)
+        for side, (rows, halo, first) in enumerate(((above, top_out, HALO - NEAR), (below, bottom_out, 0)))
+    ]
+    for s in range(2):
+
+        @pl.when(has_up)
+        def _():
+            near_down(s).wait_recv()
+
+        @pl.when(has_down)
+        def _():
+            near_up(s).wait_recv()
+
+    for keep in keeps:
+        keep.start()
 
     def local_row(ty, _):
         top = pl.multiple_of(ty * TILE, TILE)
@@ -287,52 +301,71 @@
         coarse_local.start()
         coarse_local.wait()
 
-    @pl.when(has_prev)
-    def _():
-        ahead(0).wait_recv()
-
-        @pl.when(has_up)
-        def _():
-            edge_down.wait_recv()
-
-        @pl.when(has_down)
-        def _():
-            edge_up.wait_recv()
-
-    def remote_row(ty, _):
+    def give(turn):
+        return remote(b_send, b_slots.at[j], g_s.at[turn], g_r.at[turn], at(nxt, i, lax.rem(j + turn, chans)))
+
+    def prior_row(q, _):
+        ty = jnp.where(q < 3, q + 1, jnp.where(q == 3, 0, q))
         top = pl.multiple_of(ty * TILE, TILE)
+        blocks = score_rows(
+            lambda c: own[0, c, pl.ds(pl.multiple_of(top + NEAR, NEAR), TILE), :],
+            lambda c: prior[c : c + 4, pl.ds(top, 64), :].reshape(256, 256),
+            [cs[0, ty * 8 + t] for t in range(8)],
+            [cs[1, ty * 8 + t] for t in range(8)],
+            left, right, 8,
+        )
+        for a in range(3):
+            acc[a, pl.ds(pl.multiple_of(ty * 8, 8), 8), :] = blocks[a]
+        return 0
+
+    def remote_row(n, _):
+        @pl.when(jnp.logical_and(n == 8, has_next))
+        def _():
+            b_send[...] = gather_offsets(acc_later)
+            for turn in range(chans):
+                give(turn).start()
+
+        @pl.when(jnp.logical_and(has_prev, jnp.logical_and(n == 7, has_up)))
+        def _():
+            relay_down.wait_recv()
+
+        @pl.when(jnp.logical_and(has_prev, jnp.logical_and(n == 8, has_down)))
+        def _():
+            relay_up.wait_recv()
 
         @pl.when(has_prev)
         def _():
-            @pl.when(ty < 7)
-            def _():
-                ahead(ty + 1).wait_recv()
-
+            first = jnp.where(n < 8, jnp.maximum(n - 4, 0), 5)
+            last = jnp.where(n < 4, 0, jnp.where(n < 7, n - 3, jnp.where(n == 7, 5, 8)))
+            lax.fori_loop(first, last, prior_row, 0)
+
+        ty = part_of(n)
+
+        @pl.when(jnp.logical_and(has_prev, n < 8))
+        def _():
+            ahead(ty).wait_recv()
             behind(ty).wait_send()
 
-        @pl.when(has_next)
+        @pl.when(jnp.logical_and(has_prev, jnp.logical_and(n == 0, has_up)))
+        def _():
+            relay_up.start()
+
+        @pl.when(jnp.logical_and(has_prev, jnp.logical_and(n == 1, has_down)))
+        def _():
+            relay_down.start()
+
+        @pl.when(jnp.logical_and(has_next, n < 8))
         def _():
             behind(ty).wait_recv()
             ahead(ty).wait_send()
 
-        @pl.when(ty + WINDOW < 8)
-        def _():
-            start_parts(ty + WINDOW)
-
-        @pl.when(has_prev)
-        def _():
-            blocks = score_rows(
-                lambda c: own[0, c, pl.ds(pl.multiple_of(top + NEAR, NEAR), TILE), :],
-                lambda c: prior[c : c + 4, pl.ds(top, 64), :].reshape(256, 256),
-                [cs[0, ty * 8 + t] for t in range(8)],
-                [cs[1, ty * 8 + t] for t in range(8)],
-                left, right, 8,
-            )
-            for a in range(3):
-                acc[a, pl.ds(pl.multiple_of(ty * 8, 8), 8), :] = blocks[a]
-
-        @pl.when(has_next)
-        def _():
+        @pl.when(n + WINDOW < 8)
+        def _():
+            start_parts(part_of(n + WINDOW))
+
+        @pl.when(jnp.logical_and(has_next, n < 8))
+        def _():
+            top = pl.multiple_of(ty * TILE, TILE)
             blocks = score_rows(
                 lambda c: later[c, pl.ds(top, TILE), :],
                 lambda c: own[1, 8 + c : 12 + c, pl.ds(top, 64), :].reshape(256, 256),
@@ -345,27 +378,17 @@
 
         return 0
 
-    lax.fori_loop(0, 8, remote_row, 0)
+    lax.fori_loop(0, 9, remote_row, 0)
 
     mine = gather_offsets(acc)
     q_send[...] = mine
     q_slots[j] = mine
-    b_send[...] = gather_offsets(acc_later)
 
     def share(turn):
         return remote(q_send, q_slots.at[j], d_s.at[turn], d_r.at[turn], at(k, i, lax.rem(j + turn, chans)))
 
-    def give(turn):
-        return remote(b_send, b_slots.at[j], g_s.at[turn], g_r.at[turn], at(nxt, i, lax.rem(j + turn, chans)))
-
-    for turn in range(chans):
-
-        @pl.when(has_next)
-        def _():
-            give(turn).start()
-
-        if turn:
-            share(turn).start()
+    for turn in range(1, chans):
+        share(turn).start()
 
     @pl.when(has_next)
     def _():
@@ -446,12 +469,12 @@
         new = []
         for n in range(3):
             x = fields[n]
-            above = roll(x, 8)
-            below = roll(x, 120)
+            north = roll(x, 8)
+            south = roll(x, 120)
             if n > 0:
-                above = jnp.where(tile_row == 0, roll(fields[n - 1], 72), above)
+                north = jnp.where(tile_row == 0, roll(fields[n - 1], 72), north)
             if n < 2:
-                below = jnp.where(tile_row == 7, roll(fields[n + 1], 56), below)
+                south = jnp.where(tile_row == 7, roll(fields[n + 1], 56), south)
             west = jnp.where(tile_col > 0, roll(x, 1), 0.0)
             east = jnp.where(tile_col < 7, roll(x, 127), 0.0)
             grid_row = (i + n - 1) * 8 + tile_row
@@ -461,9 +484,9 @@
                 + (tile_col > 0).astype(F32)
                 + (tile_col < 7).astype(F32)
             )
-            above = jnp.where(grid_row > 0, above, 0.0)
-            below = jnp.where(grid_row < areas * 8 - 1, below, 0.0)
-            mean = (x + (above + below + west + east)) / (1.0 + count)
+            north = jnp.where(grid_row > 0, north, 0.0)
+            south = jnp.where(grid_row < areas * 8 - 1, south, 0.0)
+            mean = (x + (north + south + west + east)) / (1.0 + count)
             new.append(mean if n == 1 else jnp.where(outside[n], mean, 0.0))
         fields = new
     field = fields[1]
@@ -486,40 +509,42 @@
         def _():
             tell(ahead_by, side).wait_send()
 
-    @pl.when(has_down)
-    def _():
-        near_down.wait_send()
-
-    @pl.when(has_up)
-    def _():
-        near_up.wait_send()
+    for s in range(2):
+
+        @pl.when(has_down)
+        def _():
+            near_down(s).wait_send()
+
+        @pl.when(has_up)
+        def _():
+            near_up(s).wait_send()
 
     @pl.when(has_prev)
     def _():
         coarse_back.wait_send()
 
-    @pl.when(jnp.logical_and(has_next, has_down))
-    def _():
-        edge_down.wait_send()
-
-    @pl.when(jnp.logical_and(has_next, has_up))
-    def _():
-        edge_up.wait_send()
-
-    for r in range(1, 4):
-
-        @pl.when(jnp.logical_and(has_down, k >= r))
-        def _():
-            far_down(r).wait_send()
-            far_up(r).wait_recv()
-
-        @pl.when(jnp.logical_and(has_up, k >= r))
-        def _():
-            far_up(r).wait_send()
-            far_down(r).wait_recv()
-
-    keep_top.wait()
-    keep_bottom.wait()
+    @pl.when(jnp.logical_and(has_prev, has_down))
+    def _():
+        relay_down.wait_send()
+
+    @pl.when(jnp.logical_and(has_prev, has_up))
+    def _():
+        relay_up.wait_send()
+
+    for n, (_, _, _, first) in enumerate(far_parts):
+
+        @pl.when(jnp.logical_and(has_down, k >= first))
+        def _():
+            far_down(n).wait_send()
+            far_up(n).wait_recv()
+
+        @pl.when(jnp.logical_and(has_up, k >= first))
+        def _():
+            far_up(n).wait_send()
+            far_down(n).wait_recv()
+
+    for keep in keeps:
+        keep.wait()
 
 
 def drift_local(devices, coarse, features):
@@ -551,10 +576,10 @@
             pltpu.VMEM((chans, 16, 128), F32),
             pltpu.VMEM((8, 128), F32),
             pltpu.VMEM((3 * secs, 8, 128), F32),
-            dma((2,)), dma((2,)), dma((2,)), dma((2, 4)), dma((2, 4)), dma((2,)), dma((2,)), dma, dma, dma,
+            dma((2,)), dma((2, 2)), dma((2, 2)), dma((2, 6)), dma((2, 6)), dma((2,)), dma((2,)), dma, dma, dma,
             dma((8,)), dma((8,)), dma((8,)), dma((8,)),
             dma((chans,)), dma((chans,)), dma((chans,)), dma((chans,)),
-            dma((secs, 3)), dma((3 * secs,)), dma((2,)),
+            dma((secs, 3)), dma((3 * secs,)), dma((2, 2)),
         ],
         compiler_params=pltpu.CompilerParams(
             collective_id=0, has_side_effects=True, vmem_limit_bytes=48 * 2**20
@@ -563,36 +588,44 @@
     )(coarse, coarse, features)
 
 
-def warp_kernel(areas, whole, frac, field, feat, top_halo, bottom_halo, out_ref, field_out, held, rows, sems):
+def warp_kernel(
+    areas, whole, frac, field, feat, top_halo, bottom_halo, out_ref, field_out, held, rows0, rows1, sems
+):
     step = pl.program_id(0)
     s = step // 8
     ty = step % 8
     i = lax.axis_index("area")
 
-    def load(part):
+    def load(section, part):
+        if part == 0:
+            halo, there = top_halo, pl.ds(0, HALO)
+        else:
+            halo, there = bottom_halo, pl.ds(HALO + 256, HALO)
         return [
-            pltpu.make_async_copy(feat.at[part], held.at[part, :, pl.ds(HALO, 256), :], sems.at[part, 0]),
-            pltpu.make_async_copy(top_halo.at[part], held.at[part, :, pl.ds(0, HALO), :], sems.at[part, 1]),
-            pltpu.make_async_copy(bottom_halo.at[part], held.at[part, :, pl.ds(HALO + 256, HALO), :], sems.at[part, 2]),
+            pltpu.make_async_copy(
+                feat.at[section, :, pl.ds(128 * part, 128), :],
+                held.at[section, :, pl.ds(HALO + 128 * part, 128), :],
+                sems.at[section, part, 0],
+            ),
+            pltpu.make_async_copy(halo.at[section], held.at[section, :, there, :], sems.at[section, part, 1]),
         ]
 
-    def wait(part):
-        for copy in load(part):
+    def start(section, part):
+        for copy in load(section, part):
+            copy.start()
+
+    def wait(section, part):
+        for copy in load(section, part):
             copy.wait()
 
-        @pl.when(i == 0)
-        def _():
-            held[part, :, pl.ds(0, HALO), :] = jnp.zeros((16, HALO, 256), BF)
-
-        @pl.when(i == areas - 1)
-        def _():
-            held[part, :, pl.ds(HALO + 256, HALO), :] = jnp.zeros((16, HALO, 256), BF)
+        @pl.when(i == (0 if part == 0 else areas - 1))
+        def _():
+            held[section, :, pl.ds(0 if part == 0 else HALO + 256, HALO), :] = jnp.zeros((16, HALO, 256), BF)
 
     @pl.when(step == 0)
     def _():
-        for part in range(2):
-            for copy in load(part):
-                copy.start()
+        start(0, 0)
+        start(0, 1)
         lane = lax.broadcasted_iota(jnp.int32, (32, 128), 1)
         row = lax.broadcasted_iota(jnp.int32, (32, 128), 0)
         spread = jnp.where(row < 16, field[0:1, :], field[1:2, :])
@@ -602,52 +635,67 @@
             spread, pick.astype(F32), precision=lax.Precision.HIGHEST, preferred_element_type=F32
         )
         field_out[...] = grid.reshape(2, 2, 8, 8)
-        wait(0)
+        wait(0, 0)
+
+    @pl.when(step == 2)
+    def _():
+        start(1, 0)
+        start(1, 1)
+        wait(0, 1)
 
     @pl.when(step == 8)
     def _():
-        wait(1)
+        wait(1, 0)
+        wait(1, 1)
 
     lane = lax.broadcasted_iota(jnp.int32, (1, 128), 1)
     lane_tile = lane // TILE
     src_col = lax.broadcasted_iota(jnp.int32, (256, 128), 0)
     base = HALO + TILE * ty
+    loaded = jnp.where(step < 2, HALO + 128, 2 * HALO + 256)
+    halves = []
     for h in range(2):
         at = step * 8 + 4 * h
         fl_row = [whole[0, at + t] for t in range(4)]
-        fl_col = [whole[1, at + t] for t in range(4)]
-        fr_row = lane_pick([frac[0, at + t] for t in range(4)], lane_tile)
-        fr_col = lane_pick([frac[1, at + t] for t in range(4)], lane_tile)
         low = jnp.minimum(jnp.minimum(fl_row[0], fl_row[1]), jnp.minimum(fl_row[2], fl_row[3]))
         high = jnp.maximum(jnp.maximum(fl_row[0], fl_row[1]), jnp.maximum(fl_row[2], fl_row[3]))
-        start = jnp.minimum((base + low) // 16 * 16, 2 * HALO + 256 - 48)
-        chunks = (base + high + TILE + 1 - start + 15) // 16
-        rel = src_col - (lane + 128 * h + lane_pick(fl_col, lane_tile))
-        weight = jnp.where(rel == 0, 1.0 - fr_col, jnp.where(rel == 1, fr_col, 0.0))
-        coarse_part = weight.astype(BF)
-        fine_part = (weight - coarse_part.astype(F32)).astype(BF)
-        mixer = jnp.concatenate([coarse_part, fine_part], 1)
-
-        def chunk(r, _):
-            at_row = pl.multiple_of(start + 16 * r, 16)
-            block = held[s, :, pl.ds(at_row, 16), :].reshape(256, 256)
+        full = (base + low) // 16 * 16
+        need = (base + high + TILE + 1 - full + 15) // 16
+        halves.append((fl_row, full, need))
+    need = jnp.maximum(halves[0][2], halves[1][2])
+
+    def run(n):
+        for h in range(2):
+            at = step * 8 + 4 * h
+            fl_row, full, _ = halves[h]
+            rows = (rows0, rows1)[h]
+            fl_col = [whole[1, at + t] for t in range(4)]
+            fr_row = lane_pick([frac[0, at + t] for t in range(4)], lane_tile)
+            fr_col = lane_pick([frac[1, at + t] for t in range(4)], lane_tile)
+            rel = src_col - (lane + 128 * h + lane_pick(fl_col, lane_tile))
+            weight = jnp.where(rel == 0, 1.0 - fr_col, jnp.where(rel == 1, fr_col, 0.0))
+            coarse_part = weight.astype(BF)
+            fine_part = (weight - coarse_part.astype(F32)).astype(BF)
+            mixer = jnp.concatenate([coarse_part, fine_part], 1)
+            start = pl.multiple_of(jnp.minimum(full, loaded - 16 * n), 16)
+            block = held[s, :, pl.ds(start, 16 * n), :].reshape(256 * n, 256)
             mixed = jnp.dot(block, mixer, preferred_element_type=F32)
             mixed = mixed[:, :128] + mixed[:, 128:]
-            rows[:, pl.ds(pl.multiple_of(16 * r, 16), 16), :] = mixed.reshape(16, 16, 128)
-            return 0
-
-        for r in range(3):
-            chunk(r, 0)
-        lax.fori_loop(3, chunks, chunk, 0)
-        offs = [base + fl_row[t] - start for t in range(4)]
-        for c in range(16):
-            upper = rows[c, pl.ds(offs[0], TILE), :]
-            lower = rows[c, pl.ds(offs[0] + 1, TILE), :]
-            for t in range(1, 4):
-                mine = lane_tile == t
-                upper = jnp.where(mine, rows[c, pl.ds(offs[t], TILE), :], upper)
-                lower = jnp.where(mine, rows[c, pl.ds(offs[t] + 1, TILE), :], lower)
-            out_ref[0, c, :, 128 * h : 128 * h + 128] = ((1.0 - fr_row) * upper + fr_row * lower).astype(BF)
+            rows[:, 0 : 16 * n, :] = mixed.reshape(16, 16 * n, 128)
+            between = [jnp.logical_and(lane_tile == t, fr_row > 0.0) for t in range(4)]
+            offs = [base + fl_row[t] - start for t in range(4)]
+            for c in range(16):
+                upper = rows[c, pl.ds(offs[0], TILE), :]
+                lower = jnp.where(between[0], rows[c, pl.ds(offs[0] + 1, TILE), :], 0.0)
+                for t in range(1, 4):
+                    upper = jnp.where(lane_tile == t, rows[c, pl.ds(offs[t], TILE), :], upper)
+                    lower = jnp.where(between[t], rows[c, pl.ds(offs[t] + 1, TILE), :], lower)
+                out_ref[0, c, :, 128 * h : 128 * h + 128] = ((1.0 - fr_row) * upper + fr_row * lower).astype(BF)
+
+    least = 0
+    for n in (4, 6, 8, 10):
+        pl.when(jnp.logical_and(need > least, need <= n))(functools.partial(run, n))
+        least = n
 
 
 def warp_local(areas, whole, frac, field, features, top_halo, bottom_halo):
@@ -667,8 +715,9 @@
         ),
         scratch_shapes=[
             pltpu.VMEM((2, 16, 2 * HALO + 256, 256), BF),
-            pltpu.VMEM((16, 176, 128), F32),
-            pltpu.SemaphoreType.DMA((2, 3)),
+            pltpu.VMEM((16, 160, 128), F32),
+            pltpu.VMEM((16, 160, 128), F32),
+            pltpu.SemaphoreType.DMA((2, 2, 2)),
         ],
         compiler_params=pltpu.CompilerParams(vmem_limit_bytes=48 * 2**20),
         name="warp",

time: 114 us -> 95.1 us (0.83)
  Pallas kernels: 112 us -> 92.3 us
    pallas_call x1, Pallas kernels: 27 us -> 16.2 us  [warp_local(): pl.pallas_call(functools.partial(warp_kernel, areas), grid=(16,), out_sha...]
    pallas_call x1, Pallas kernels: 85.1 us -> 76.1 us  [drift_local(): pl.pallas_call(functools.partial(drift_kernel, devices), out_shape=(small...]
where the time goes in v3:
time: 95.1 us; the launch traced here: 93.8 us
  Pallas kernels  92.3 us (97%)
    pallas_call x1, Pallas kernels, drift_local(): pl.pallas_call(functools.partial(drift_kernel, devices), out_shape=(small...  76.1 us
    pallas_call x1, Pallas kernels, warp_local(): pl.pallas_call(functools.partial(warp_kernel, areas), grid=(16,), out_sha...  16.2 us

profile of v3, /device:TPU:197, one launch (start us, length us, event | category | flops | bytes accessed | tf_op | source)
XLA Modules:
  0.0 93.8 jit_solution(14402564820370770788)
XLA Ops:
  0.6 0.8 reshape.7.cs.cv
  1.4 76.1 %drift.1 = (f32[2,128]{1,0:T(2,128)S(1)}, s32[2,128]{1,0:T(2,128)S(1)}, f32[2,128]{1,0:T(2,128)S(1)}, bf16[2,16,64,256]{3,2,1,0:T(8,128)(2,1)S(1)}, bf16[2,16,64,256]{3,2,1,0:T(8,128)(2,1)S(1)}) custom-call(s32[2,128]{1,0:T(2,128)S(1)} %reshape.7.cs.cv, s32[2,128]{1,0:T(2,128)S(1)} %reshape.7.cs.cv, bf16[2,16,256,256]{3,2,1,0:T(8,128)(2,1)} %feat.3), custom_call_target="tpu_custom_call" | custom-call | tf_op jit(solution)/shard_map/drift/pallas_call | solution.py:558
  77.6 16.2 %warp.1 = (bf16[2,16,256,256]{3,2,1,0:T(8,128)(2,1)}, f32[2,2,8,8]{3,2,1,0:T(8,128)}) custom-call(s32[2,128]{1,0:T(2,128)S(1)} %get-tuple-element.7.whole, f32[2,128]{1,0:T(2,128)S(1)} %get-tuple-element.8.frac, f32[2,128]{1,0:T(2,128)S(1)} %get-tuple-element.9.field, bf16[2,16,256,256]{3,2,1,0:T(8,128)(2,1)} %feat.3, ...), custom_call_target="tpu_custom_call" | custom-call | tf_op jit(solution)/shard_map/warp/pallas_call | solution.py:704

commit v4 on v3

--- a/solution.py
+++ b/solution.py
@@ -26,7 +26,7 @@
 
 
 NEAR = 16
-WINDOW = 8
+WINDOW = 5
 
 
 def score_rows(f_rows, window, coarse_row, coarse_col, left, right, count):
@@ -91,9 +91,9 @@
 
 
 def drift_kernel(
-    devices, cs, cv, feat,
+    devices, cs, cv4, feat,
     field_out, whole_out, frac_out, top_out, bottom_out,
-    own, prior, later, later_coarse, later_cs, left, right, acc, acc_later,
+    own, prior, later, cv, later_coarse, later_cs, left, right, lefts, rights, acc, acc_later,
     q_send, b_send, q_slots, b_slots, e_send, e_slots,
     load_sem, near_s, near_r, far_s, far_r, edge_s, edge_r, cc_s, cc_r, cc_l,
     a_s, a_r, b_s, b_r, d_s, d_r, g_s, g_r, e_s, e_r, keep_sem,
@@ -121,6 +121,15 @@
     for load in loads:
         load.start()
 
+    grid_row = lax.broadcasted_iota(jnp.int32, (32, 128), 0) % 16
+    grid_lane = lax.broadcasted_iota(jnp.int32, (32, 128), 1)
+    column = lax.broadcasted_iota(jnp.int32, (8, 128), 1) % 8 == lax.broadcasted_iota(jnp.int32, (8, 128), 0)
+    spread = jnp.dot(
+        cv4[...].reshape(32, 8).astype(F32), column.astype(F32), precision=lax.Precision.HIGHEST, preferred_element_type=F32
+    )
+    spread = jnp.where(grid_lane // 8 == grid_row, spread, 0.0)
+    cv[...] = jnp.sum(spread.reshape(2, 16, 128), axis=1).astype(jnp.int32)
+
     barrier = pltpu.get_barrier_semaphore()
     for other in range(secs):
         for side, there in ((-1, has_up), (0, True), (1, has_down)):
@@ -208,14 +217,19 @@
         def _():
             behind(c).start()
 
-    def start_far():
-        for n, (_, _, _, first) in enumerate(far_parts):
-
-            @pl.when(jnp.logical_and(has_down, k >= first))
+    even = lax.rem(i, 2) == 0
+
+    def start_far(inside, chosen=range(6)):
+        goes_down = jnp.logical_and(has_down, even if inside else jnp.logical_not(even))
+        goes_up = jnp.logical_and(has_up, jnp.logical_not(even) if inside else even)
+        for n in chosen:
+            first = far_parts[n][3]
+
+            @pl.when(jnp.logical_and(goes_down, k >= first))
             def _():
                 far_down(n).start()
 
-            @pl.when(jnp.logical_and(has_up, k >= first))
+            @pl.when(jnp.logical_and(goes_up, k >= first))
             def _():
                 far_up(n).start()
 
@@ -239,9 +253,7 @@
     for n in range(WINDOW):
         start_parts(part_of(n))
 
-    @pl.when(jnp.logical_not(has_next))
-    def _():
-        start_far()
+    start_far(True)
 
     @pl.when(jnp.logical_not(has_up))
     def _():
@@ -283,8 +295,8 @@
         blocks = score_rows(
             lambda c: own[1, c, pl.ds(pl.multiple_of(top + NEAR, NEAR), TILE), :],
             lambda c: own[0, c : c + 4, pl.ds(top, 64), :].reshape(256, 256),
-            [cs[0, 64 + ty * 8 + t] for t in range(8)],
-            [cs[1, 64 + ty * 8 + t] for t in range(8)],
+            [cs[0, 1, ty, t] for t in range(8)],
+            [cs[1, 1, ty, t] for t in range(8)],
             left, right, 16,
         )
         for a in range(3):
@@ -304,18 +316,18 @@
     def give(turn):
         return remote(b_send, b_slots.at[j], g_s.at[turn], g_r.at[turn], at(nxt, i, lax.rem(j + turn, chans)))
 
-    def prior_row(q, _):
-        ty = jnp.where(q < 3, q + 1, jnp.where(q == 3, 0, q))
-        top = pl.multiple_of(ty * TILE, TILE)
+    def prior_row(q, room=0):
+        ty = q if isinstance(q, int) else jnp.where(q < 3, q + 1, jnp.where(q == 3, 0, q))
+        top = ty * TILE if isinstance(ty, int) else pl.multiple_of(ty * TILE, TILE)
         blocks = score_rows(
-            lambda c: own[0, c, pl.ds(pl.multiple_of(top + NEAR, NEAR), TILE), :],
+            lambda c: own[0, c, pl.ds(top + NEAR if isinstance(ty, int) else pl.multiple_of(top + NEAR, NEAR), TILE), :],
             lambda c: prior[c : c + 4, pl.ds(top, 64), :].reshape(256, 256),
-            [cs[0, ty * 8 + t] for t in range(8)],
-            [cs[1, ty * 8 + t] for t in range(8)],
-            left, right, 8,
+            [cs[0, 0, ty, t] for t in range(8)],
+            [cs[1, 0, ty, t] for t in range(8)],
+            lefts.at[room], rights.at[room], 8,
         )
         for a in range(3):
-            acc[a, pl.ds(pl.multiple_of(ty * 8, 8), 8), :] = blocks[a]
+            acc[a, pl.ds(ty * 8 if isinstance(ty, int) else pl.multiple_of(ty * 8, 8), 8), :] = blocks[a]
         return 0
 
     def remote_row(n, _):
@@ -333,11 +345,15 @@
         def _():
             relay_up.wait_recv()
 
-        @pl.when(has_prev)
-        def _():
-            first = jnp.where(n < 8, jnp.maximum(n - 4, 0), 5)
-            last = jnp.where(n < 4, 0, jnp.where(n < 7, n - 3, jnp.where(n == 7, 5, 8)))
-            lax.fori_loop(first, last, prior_row, 0)
+        @pl.when(jnp.logical_and(has_prev, n < 8))
+        def _():
+            last = jnp.where(n < 4, 0, jnp.where(n < 7, n - 3, 5))
+            lax.fori_loop(jnp.maximum(n - 4, 0), last, lambda q, _: prior_row(q), 0)
+
+        @pl.when(jnp.logical_and(has_prev, n == 8))
+        def _():
+            for room in range(3):
+                prior_row(5 + room, room)
 
         ty = part_of(n)
 
@@ -362,6 +378,10 @@
         @pl.when(n + WINDOW < 8)
         def _():
             start_parts(part_of(n + WINDOW))
+
+        @pl.when(jnp.logical_and(jnp.logical_not(has_next), n == 8 - WINDOW))
+        def _():
+            start_far(False)
 
         @pl.when(jnp.logical_and(has_next, n < 8))
         def _():
@@ -392,7 +412,7 @@
 
     @pl.when(has_next)
     def _():
-        start_far()
+        start_far(False, (0, 1, 2))
 
     for turn in range(chans):
         if turn:
@@ -440,6 +460,10 @@
         @pl.when(fits)
         def _():
             tell(ahead_by, side).start()
+
+    @pl.when(has_next)
+    def _():
+        start_far(False, (3, 4, 5))
 
     def hear(sec, side):
         return remote(
@@ -565,9 +589,12 @@
             pltpu.VMEM((8, 256 + 2 * NEAR, 256), BF),
             pltpu.VMEM((8, 256, 256), BF),
             pltpu.VMEM((2, 128), jnp.int32),
+            pltpu.VMEM((2, 128), jnp.int32),
             pltpu.SMEM((2, 128), jnp.int32),
             pltpu.VMEM((2, 128, 2048), BF),
             pltpu.VMEM((2, 192, 2048), BF),
+            pltpu.VMEM((3, 2, 128, 1024), BF),
+            pltpu.VMEM((3, 2, 192, 1024), BF),
             pltpu.VMEM((3, 128, 192), F32),
             pltpu.VMEM((3, 128, 192), F32),
             pltpu.VMEM((16, 128), F32),
@@ -589,11 +616,11 @@
 
 
 def warp_kernel(
-    areas, whole, frac, field, feat, top_halo, bottom_halo, out_ref, field_out, held, rows0, rows1, sems
+    areas, whole, frac, field, feat, top_halo, bottom_halo, out_ref, field_out, held, rows_all, sems
 ):
     step = pl.program_id(0)
-    s = step // 8
-    ty = step % 8
+    s = step // 4
+    ty0 = step % 4 * 2
     i = lax.axis_index("area")
 
     def load(section, part):
@@ -637,13 +664,13 @@
         field_out[...] = grid.reshape(2, 2, 8, 8)
         wait(0, 0)
 
-    @pl.when(step == 2)
+    @pl.when(step == 1)
     def _():
         start(1, 0)
         start(1, 1)
         wait(0, 1)
 
-    @pl.when(step == 8)
+    @pl.when(step == 4)
     def _():
         wait(1, 0)
         wait(1, 1)
@@ -651,24 +678,23 @@
     lane = lax.broadcasted_iota(jnp.int32, (1, 128), 1)
     lane_tile = lane // TILE
     src_col = lax.broadcasted_iota(jnp.int32, (256, 128), 0)
-    base = HALO + TILE * ty
-    loaded = jnp.where(step < 2, HALO + 128, 2 * HALO + 256)
-    halves = []
-    for h in range(2):
-        at = step * 8 + 4 * h
-        fl_row = [whole[0, at + t] for t in range(4)]
-        low = jnp.minimum(jnp.minimum(fl_row[0], fl_row[1]), jnp.minimum(fl_row[2], fl_row[3]))
-        high = jnp.maximum(jnp.maximum(fl_row[0], fl_row[1]), jnp.maximum(fl_row[2], fl_row[3]))
-        full = (base + low) // 16 * 16
-        need = (base + high + TILE + 1 - full + 15) // 16
-        halves.append((fl_row, full, need))
-    need = jnp.maximum(halves[0][2], halves[1][2])
+    parts = []
+    need = jnp.int32(0)
+    for q in range(2):
+        base = HALO + TILE * (ty0 + q)
+        for h in range(2):
+            at = s * 64 + (ty0 + q) * 8 + 4 * h
+            fl_row = [whole[0, at + t] for t in range(4)]
+            low = jnp.minimum(jnp.minimum(fl_row[0], fl_row[1]), jnp.minimum(fl_row[2], fl_row[3]))
+            high = jnp.maximum(jnp.maximum(fl_row[0], fl_row[1]), jnp.maximum(fl_row[2], fl_row[3]))
+            full = (base + low) // 16 * 16
+            need = jnp.maximum(need, (base + high + TILE + 1 - full + 15) // 16)
+            parts.append((q, h, at, base, fl_row, full))
+    loaded = jnp.where(jnp.logical_and(s == 0, ty0 < 2), 192, 2 * HALO + 256)
 
     def run(n):
-        for h in range(2):
-            at = step * 8 + 4 * h
-            fl_row, full, _ = halves[h]
-            rows = (rows0, rows1)[h]
+        for q, h, at, base, fl_row, full in parts:
+            rows = rows_all.at[2 * q + h]
             fl_col = [whole[1, at + t] for t in range(4)]
             fr_row = lane_pick([frac[0, at + t] for t in range(4)], lane_tile)
             fr_col = lane_pick([frac[1, at + t] for t in range(4)], lane_tile)
@@ -690,7 +716,9 @@
                 for t in range(1, 4):
                     upper = jnp.where(lane_tile == t, rows[c, pl.ds(offs[t], TILE), :], upper)
                     lower = jnp.where(between[t], rows[c, pl.ds(offs[t] + 1, TILE), :], lower)
-                out_ref[0, c, :, 128 * h : 128 * h + 128] = ((1.0 - fr_row) * upper + fr_row * lower).astype(BF)
+                out_ref[0, c, TILE * q : TILE * q + TILE, 128 * h : 128 * h + 128] = (
+                    (1.0 - fr_row) * upper + fr_row * lower
+                ).astype(BF)
 
     least = 0
     for n in (4, 6, 8, 10):
@@ -703,20 +731,19 @@
     hbm = pl.BlockSpec(memory_space=pl.ANY)
     return pl.pallas_call(
         functools.partial(warp_kernel, areas),
-        grid=(16,),
+        grid=(8,),
         out_shape=(
             jax.ShapeDtypeStruct((2, 16, 256, 256), BF),
             jax.ShapeDtypeStruct((2, 2, 8, 8), F32),
         ),
         in_specs=[sm, sm, pl.BlockSpec(memory_space=pltpu.VMEM), hbm, hbm, hbm],
         out_specs=(
-            pl.BlockSpec((1, 16, TILE, 256), lambda g: (g // 8, 0, g % 8, 0)),
+            pl.BlockSpec((1, 16, 2 * TILE, 256), lambda g: (g // 4, 0, g % 4, 0)),
             pl.BlockSpec(memory_space=pltpu.VMEM),
         ),
         scratch_shapes=[
             pltpu.VMEM((2, 16, 2 * HALO + 256, 256), BF),
-            pltpu.VMEM((16, 160, 128), F32),
-            pltpu.VMEM((16, 160, 128), F32),
+            pltpu.VMEM((4, 16, 160, 128), F32),
             pltpu.SemaphoreType.DMA((2, 2, 2)),
         ],
         compiler_params=pltpu.CompilerParams(vmem_limit_bytes=48 * 2**20),
@@ -725,7 +752,7 @@
 
 
 def local(devices, features, coarse):
-    field, whole, frac, top_halo, bottom_halo = drift_local(devices, coarse.reshape(2, 128), features)
+    field, whole, frac, top_halo, bottom_halo = drift_local(devices, coarse, features)
     return warp_local(devices[1], whole, frac, field, features, top_halo, bottom_halo)
 
 

time: 95.1 us -> 94.4 us (level)
  the two profiles are of different devices: /device:TPU:197 before, /device:TPU:161 now
where the time goes in v4:
time: 94.4 us; the launch traced here: 94.3 us
  Pallas kernels  92.8 us (98%)
    pallas_call x1, Pallas kernels, drift_local(): pl.pallas_call(functools.partial(drift_kernel, devices), out_shape=(small...  76.8 us
    pallas_call x1, Pallas kernels, warp_local(): pl.pallas_call(functools.partial(warp_kernel, areas), grid=(8,), out_shap...  15.9 us

profile of v4, /device:TPU:161, one launch (start us, length us, event | category | flops | bytes accessed | tf_op | source)
XLA Modules:
  0.0 94.3 jit_solution(1220848641350242924)
XLA Ops:
  0.6 0.0 copy-start
  0.6 0.7 copy-done
  1.3 76.8 %drift.1 = (f32[2,128]{1,0:T(2,128)S(1)}, s32[2,128]{1,0:T(2,128)S(1)}, f32[2,128]{1,0:T(2,128)S(1)}, bf16[2,16,64,256]{3,2,1,0:T(8,128)(2,1)S(1)}, bf16[2,16,64,256]{3,2,1,0:T(8,128)(2,1)S(1)}) custom-call(s32[2,2,8,8]{3,2,1,0:T(8,128)S(1)} %copy-done, s32[2,2,8,8]{3,2,1,0:T(8,128)S(1)} %copy-done, bf16[2,16,256,256]{3,2,1,0:T(8,128)(2,1)} %feat.3), custom_call_target="tpu_custom_call" | custom-call | tf_op jit(solution)/shard_map/drift/pallas_call | solution.py:582
  78.2 15.9 %warp.1 = (bf16[2,16,256,256]{3,2,1,0:T(8,128)(2,1)}, f32[2,2,8,8]{3,2,1,0:T(8,128)}) custom-call(s32[2,128]{1,0:T(2,128)S(1)} %get-tuple-element.7.whole, f32[2,128]{1,0:T(2,128)S(1)} %get-tuple-element.8.frac, f32[2,128]{1,0:T(2,128)S(1)} %get-tuple-element.9.field, bf16[2,16,256,256]{3,2,1,0:T(8,128)(2,1)} %feat.3, ...), custom_call_target="tpu_custom_call" | custom-call | tf_op jit(solution)/shard_map/warp/pallas_call | solution.py:732
Async XLA Ops:
  0.6 0.7 copy-start

commit v5 on v4

--- a/solution.py
+++ b/solution.py
@@ -121,6 +121,125 @@
     for load in loads:
         load.start()
 
+    barrier = pltpu.get_barrier_semaphore()
+    for other in range(secs):
+        for side, there in ((-1, has_up), (0, True), (1, has_down)):
+            fits = jnp.logical_and(there, jnp.logical_or(side != 0, k != other))
+
+            @pl.when(fits)
+            def _():
+                pl.semaphore_signal(barrier, inc=1, device_id=at(other, i + side, j), device_id_type=MESH)
+
+    for step, there in ((-1, has_prev), (0, True), (1, has_next)):
+        for turn in range(1, chans):
+
+            @pl.when(there)
+            def _():
+                pl.semaphore_signal(
+                    barrier, inc=1, device_id=at(k + step, i, lax.rem(j + turn, chans)), device_id_type=MESH
+                )
+
+    one = lambda flag: jnp.where(flag, 1, 0)
+    pl.semaphore_wait(
+        barrier,
+        secs * (1 + one(has_up) + one(has_down)) - 1 + (chans - 1) * (1 + one(has_prev) + one(has_next)),
+    )
+
+    heads, tails = pl.ds(0, NEAR), pl.ds(256 - NEAR, NEAR)
+    above, below = pl.ds(0, NEAR), pl.ds(NEAR + 256, NEAR)
+    near_chans = (pl.ds(0, 16), pl.ds(8, 8))
+
+    def near_down(s):
+        return remote(
+            feat.at[s, near_chans[s], tails, :], own.at[s, near_chans[s], above, :], near_s.at[0, s], near_r.at[0, s], at(k, down, j)
+        )
+
+    def near_up(s):
+        return remote(
+            feat.at[s, near_chans[s], heads, :], own.at[s, near_chans[s], below, :], near_s.at[1, s], near_r.at[1, s], at(k, up, j)
+        )
+
+    relay_up = remote(
+        prior.at[:, pl.ds(NEAR, NEAR), :], prior.at[:, below, :], edge_s.at[1], edge_r.at[1], at(k, up, j)
+    )
+    relay_down = remote(
+        prior.at[:, pl.ds(256, NEAR), :], prior.at[:, above, :], edge_s.at[0], edge_r.at[0], at(k, down, j)
+    )
+    coarse_back = remote(cv, later_coarse, cc_s, cc_r, at(prv, i, j))
+
+    far_parts = [(1, 0, 8, 0), (0, 1, 16, 2), (1, 1, 16, 1), (0, 2, 16, 3), (1, 2, 16, 2), (1, 3, 16, 3)]
+
+    def far_down(n):
+        s, r, channels, _ = far_parts[n]
+        return remote(
+            feat.at[s, pl.ds(0, channels), pl.ds(240 - 16 * r, 16), :],
+            top_out.at[s, pl.ds(0, channels), pl.ds(HALO - 16 * (r + 1), 16), :],
+            far_s.at[0, n], far_r.at[0, n], at(k, down, j),
+        )
+
+    def far_up(n):
+        s, r, channels, _ = far_parts[n]
+        return remote(
+            feat.at[s, pl.ds(0, channels), pl.ds(16 * r, 16), :],
+            bottom_out.at[s, pl.ds(0, channels), pl.ds(16 * r, 16), :],
+            far_s.at[1, n], far_r.at[1, n], at(k, up, j),
+        )
+
+    def ahead(c):
+        return remote(
+            feat.at[1, pl.ds(0, 8), pl.ds(pl.multiple_of(TILE * c, TILE), TILE), :],
+            prior.at[:, pl.ds(pl.multiple_of(NEAR + TILE * c, NEAR), TILE), :],
+            a_s.at[c], a_r.at[c], at(nxt, i, j),
+        )
+
+    def behind(c):
+        return remote(
+            feat.at[0, pl.ds(8, 8), pl.ds(pl.multiple_of(TILE * c, TILE), TILE), :],
+            later.at[:, pl.ds(pl.multiple_of(TILE * c, TILE), TILE), :],
+            b_s.at[c], b_r.at[c], at(prv, i, j),
+        )
+
+    def start_parts(c):
+        @pl.when(has_next)
+        def _():
+            ahead(c).start()
+
+        @pl.when(has_prev)
+        def _():
+            behind(c).start()
+
+    even = lax.rem(i, 2) == 0
+
+    def start_far(inside, chosen=range(6)):
+        goes_down = jnp.logical_and(has_down, even if inside else jnp.logical_not(even))
+        goes_up = jnp.logical_and(has_up, jnp.logical_not(even) if inside else even)
+        for n in chosen:
+            first = far_parts[n][3]
+
+            @pl.when(jnp.logical_and(goes_down, k >= first))
+            def _():
+                far_down(n).start()
+
+            @pl.when(jnp.logical_and(goes_up, k >= first))
+            def _():
+                far_up(n).start()
+
+    def part_of(n):
+        return jnp.where(n == 0, 0, jnp.where(n == 1, 7, n - 1))
+
+    for s in range(2):
+
+        @pl.when(has_down)
+        def _():
+            near_down(s).start()
+
+        @pl.when(has_up)
+        def _():
+            near_up(s).start()
+
+    for n in range(WINDOW):
+        start_parts(part_of(n))
+
     grid_row = lax.broadcasted_iota(jnp.int32, (32, 128), 0) % 16
     grid_lane = lax.broadcasted_iota(jnp.int32, (32, 128), 1)
     column = lax.broadcasted_iota(jnp.int32, (8, 128), 1) % 8 == lax.broadcasted_iota(jnp.int32, (8, 128), 0)
@@ -130,128 +249,9 @@
     spread = jnp.where(grid_lane // 8 == grid_row, spread, 0.0)
     cv[...] = jnp.sum(spread.reshape(2, 16, 128), axis=1).astype(jnp.int32)
 
-    barrier = pltpu.get_barrier_semaphore()
-    for other in range(secs):
-        for side, there in ((-1, has_up), (0, True), (1, has_down)):
-            fits = jnp.logical_and(there, jnp.logical_or(side != 0, k != other))
-
-            @pl.when(fits)
-            def _():
-                pl.semaphore_signal(barrier, inc=1, device_id=at(other, i + side, j), device_id_type=MESH)
-
-    for step, there in ((-1, has_prev), (0, True), (1, has_next)):
-        for turn in range(1, chans):
-
-            @pl.when(there)
-            def _():
-                pl.semaphore_signal(
-                    barrier, inc=1, device_id=at(k + step, i, lax.rem(j + turn, chans)), device_id_type=MESH
-                )
-
-    one = lambda flag: jnp.where(flag, 1, 0)
-    pl.semaphore_wait(
-        barrier,
-        secs * (1 + one(has_up) + one(has_down)) - 1 + (chans - 1) * (1 + one(has_prev) + one(has_next)),
-    )
-
-    heads, tails = pl.ds(0, NEAR), pl.ds(256 - NEAR, NEAR)
-    above, below = pl.ds(0, NEAR), pl.ds(NEAR + 256, NEAR)
-    near_chans = (pl.ds(0, 16), pl.ds(8, 8))
-
-    def near_down(s):
-        return remote(
-            feat.at[s, near_chans[s], tails, :], own.at[s, near_chans[s], above, :], near_s.at[0, s], near_r.at[0, s], at(k, down, j)
-        )
-
-    def near_up(s):
-        return remote(
-            feat.at[s, near_chans[s], heads, :], own.at[s, near_chans[s], below, :], near_s.at[1, s], near_r.at[1, s], at(k, up, j)
-        )
-
-    relay_up = remote(
-        prior.at[:, pl.ds(NEAR, NEAR), :], prior.at[:, below, :], edge_s.at[1], edge_r.at[1], at(k, up, j)
-    )
-    relay_down = remote(
-        prior.at[:, pl.ds(256, NEAR), :], prior.at[:, above, :], edge_s.at[0], edge_r.at[0], at(k, down, j)
-    )
-    coarse_back = remote(cv, later_coarse, cc_s, cc_r, at(prv, i, j))
-
-    far_parts = [(1, 0, 8, 0), (0, 1, 16, 2), (1, 1, 16, 1), (0, 2, 16, 3), (1, 2, 16, 2), (1, 3, 16, 3)]
-
-    def far_down(n):
-        s, r, channels, _ = far_parts[n]
-        return remote(
-            feat.at[s, pl.ds(0, channels), pl.ds(240 - 16 * r, 16), :],
-            top_out.at[s, pl.ds(0, channels), pl.ds(HALO - 16 * (r + 1), 16), :],
-            far_s.at[0, n], far_r.at[0, n], at(k, down, j),
-        )
-
-    def far_up(n):
-        s, r, channels, _ = far_parts[n]
-        return remote(
-            feat.at[s, pl.ds(0, channels), pl.ds(16 * r, 16), :],
-            bottom_out.at[s, pl.ds(0, channels), pl.ds(16 * r, 16), :],
-            far_s.at[1, n], far_r.at[1, n], at(k, up, j),
-        )
-
-    def ahead(c):
-        return remote(
-            feat.at[1, pl.ds(0, 8), pl.ds(pl.multiple_of(TILE * c, TILE), TILE), :],
-            prior.at[:, pl.ds(pl.multiple_of(NEAR + TILE * c, NEAR), TILE), :],
-            a_s.at[c], a_r.at[c], at(nxt, i, j),
-        )
-
-    def behind(c):
-        return remote(
-            feat.at[0, pl.ds(8, 8), pl.ds(pl.multiple_of(TILE * c, TILE), TILE), :],
-            later.at[:, pl.ds(pl.multiple_of(TILE * c, TILE), TILE), :],
-            b_s.at[c], b_r.at[c], at(prv, i, j),
-        )
-
-    def start_parts(c):
-        @pl.when(has_next)
-        def _():
-            ahead(c).start()
-
-        @pl.when(has_prev)
-        def _():
-            behind(c).start()
-
-    even = lax.rem(i, 2) == 0
-
-    def start_far(inside, chosen=range(6)):
-        goes_down = jnp.logical_and(has_down, even if inside else jnp.logical_not(even))
-        goes_up = jnp.logical_and(has_up, jnp.logical_not(even) if inside else even)
-        for n in chosen:
-            first = far_parts[n][3]
-
-            @pl.when(jnp.logical_and(goes_down, k >= first))
-            def _():
-                far_down(n).start()
-
-            @pl.when(jnp.logical_and(goes_up, k >= first))
-            def _():
-                far_up(n).start()
-
-    def part_of(n):
-        return jnp.where(n == 0, 0, jnp.where(n == 1, 7, n - 1))
-
-    for s in range(2):
-
-        @pl.when(has_down)
-        def _():
-            near_down(s).start()
-
-        @pl.when(has_up)
-        def _():
-            near_up(s).start()
-
     @pl.when(has_prev)
     def _():
         coarse_back.start()
-
-    for n in range(WINDOW):
-        start_parts(part_of(n))
 
     start_far(True)
 
@@ -378,6 +378,10 @@
         @pl.when(n + WINDOW < 8)
         def _():
             start_parts(part_of(n + WINDOW))
+
+        @pl.when(jnp.logical_and(has_next, n == 8 - WINDOW))
+        def _():
+            start_far(False, (2,))
 
         @pl.when(jnp.logical_and(jnp.logical_not(has_next), n == 8 - WINDOW))
         def _():
@@ -412,7 +416,7 @@
 
     @pl.when(has_next)
     def _():
-        start_far(False, (0, 1, 2))
+        start_far(False, (0, 1))
 
     for turn in range(chans):
         if turn:
@@ -746,7 +750,7 @@
             pltpu.VMEM((4, 16, 160, 128), F32),
             pltpu.SemaphoreType.DMA((2, 2, 2)),
         ],
-        compiler_params=pltpu.CompilerParams(vmem_limit_bytes=48 * 2**20),
+        compiler_params=pltpu.CompilerParams(vmem_limit_bytes=24 * 2**20),
         name="warp",
     )(whole, frac, field, features, top_halo, bottom_halo)
 

time: 94.4 us -> 92.9 us (0.984)
  the two profiles are of different devices: /device:TPU:161 before, /device:TPU:197 now
where the time goes in v5:
time: 92.9 us; the launch traced here: 92.4 us
  Pallas kernels  90.7 us (98%)
    pallas_call x1, Pallas kernels, drift_local(): pl.pallas_call(functools.partial(drift_kernel, devices), out_shape=(small...  73.7 us
    pallas_call x1, Pallas kernels, warp_local(): pl.pallas_call(functools.partial(warp_kernel, areas), grid=(8,), out_shap...  17 us

profile of v5, /device:TPU:197, one launch (start us, length us, event | category | flops | bytes accessed | tf_op | source)
XLA Modules:
  0.0 92.4 jit_solution(10885009267390230660)
XLA Ops:
  0.6 0.0 copy-start
  0.6 0.0 copy-start.1
  0.6 0.9 copy-done.1
  1.5 73.7 %drift.1 = (f32[2,128]{1,0:T(2,128)S(1)}, s32[2,128]{1,0:T(2,128)S(1)}, f32[2,128]{1,0:T(2,128)S(1)}, bf16[2,16,64,256]{3,2,1,0:T(8,128)(2,1)S(1)}, bf16[2,16,64,256]{3,2,1,0:T(8,128)(2,1)S(1)}) custom-call(s32[2,2,8,8]{3,2,1,0:T(8,128)S(1)} %copy-done.1, s32[2,2,8,8]{3,2,1,0:T(8,128)S(1)} %copy-done.1, bf16[2,16,256,256]{3,2,1,0:T(8,128)(2,1)} %feat.3), custom_call_target="tpu_custom_call" | custom-call | tf_op jit(solution)/shard_map/drift/pallas_call | solution.py:586
  75.2 0.0 copy-done
  75.2 17.0 %warp.1 = (bf16[2,16,256,256]{3,2,1,0:T(8,128)(2,1)}, f32[2,2,8,8]{3,2,1,0:T(8,128)}) custom-call(s32[2,128]{1,0:T(2,128)S(1)} %get-tuple-element.7.whole, f32[2,128]{1,0:T(2,128)S(1)} %get-tuple-element.8.frac, f32[2,128]{1,0:T(2,128)S(1)} %get-tuple-element.9.field, bf16[2,16,256,256]{3,2,1,0:T(8,128)(2,1)S(1)} %copy-done, ...), custom_call_target="tpu_custom_call" | custom-call | tf_op jit(solution)/shard_map/warp/pallas_call | solution.py:736
Async XLA Ops:
  0.6 74.6 %copy-start = (bf16[2,16,256,256]{3,2,1,0:T(8,128)(2,1)S(1)}, bf16[2,16,256,256]{3,2,1,0:T(8,128)(2,1)}, u32[]{:S(2)}) copy-start(bf16[2,16,256,256]{3,2,1,0:T(8,128)(2,1)} %feat.3) | copy-start | bytes 12582916
  0.6 0.9 copy-start.1
